TPU v7x, 128 devices: a whole 4x4x4 slice. The times are simulated.
128 devices in a mesh: fsdp: 16 (over z, y), tp: 8 (over x, core).
Axes of the slice: x: 4, y: 4, z: 4, core: 2. Of those that a mesh axis runs over, the one named last changes fastest.
Arguments:
- gradient: bfloat16 [28672, 8192], P('fsdp', 'tp'), may hold values from -6 to 6
- momentum: float32 [28672, 8192], P('fsdp', 'tp'), may hold values from -36 to 36
- basis: float32 [8192, 256], P('tp'), may hold values from -0.0625 to 0.0625
Outputs:
- new_momentum: float32 [28672, 8192], P('fsdp', 'tp')
- new_basis: float32 [8192, 256], P('tp')
- update: bfloat16 [28672, 8192], P('fsdp', 'tp')
All inputs are finite; a program needn't handle non-finite values.
Results may differ from a plain program's by a relative error of at most 0.0015.
Values sent between devices are 32-bit elements; how exact they have to be, the bound alone decides.
A program may use at most 128 MiB of HBM per device.

v0:
```python
import jax
import jax.numpy as jnp
from jax import lax
from jax.sharding import PartitionSpec as P

ROWS = 28672
COLS = 8192
RANK = 256


HIGH = lax.Precision.HIGHEST


def transposed(left, right):
    return lax.dot_general(
        left, right, (((0,), (0,)), ((), ())), precision=HIGH, preferred_element_type=jnp.float32
    )


def body(gradient, momentum, basis):
    blend = momentum + gradient.astype(jnp.float32)
    partial_proj = jnp.dot(blend, basis, precision=HIGH, preferred_element_type=jnp.float32)
    projected = lax.psum(partial_proj, "tp")
    gram = lax.psum(transposed(projected, projected), "fsdp")
    factor = jnp.linalg.cholesky(gram)
    ortho = lax.linalg.triangular_solve(
        factor, projected, left_side=False, lower=True, transpose_a=True
    )
    back = lax.psum(transposed(blend, ortho), "fsdp")
    new_momentum = blend - 0.05 * jnp.dot(
        ortho, back.T, precision=HIGH, preferred_element_type=jnp.float32
    )
    squares = lax.psum(jnp.sum(back * back, axis=0), "tp")
    new_basis = back * lax.rsqrt(squares + 1e-06)
    scale = (ROWS * COLS / RANK) ** 0.5
    update = (
        scale * jnp.dot(ortho, new_basis.T, precision=HIGH, preferred_element_type=jnp.float32)
    ).astype(jnp.bfloat16)
    return (new_momentum, new_basis, update)


def solution(mesh):
    placed = (P("fsdp", "tp"), P("fsdp", "tp"), P("tp", None))
    return jax.shard_map(
        body,
        mesh=mesh,
        in_specs=placed,
        out_specs=(P("fsdp", "tp"), P("tp", None), P("fsdp", "tp")),
        check_vma=False,
    )
```

profile of v0, /device:TPU:1, one launch (start us, length us, event | category | flops | bytes accessed | tf_op | source)
XLA Modules:
  0.0 398.1 jit_solution(16293851243359185415)
XLA Ops:
  7.2 1.2 copy-done
  8.4 10.0 %fusion.1 = f32[1792,256]{1,0:T(8,128)} fusion(f32[1024,256]{1,0:T(8,128)S(1)} %copy-done, f32[1792,1024]{1,0:T(8,128)} %param.4, bf16[1792,1024]{1,0:T(8,128)(2,1)} %param.3), kind=kOutput, calls=%fused_computation.6 | convolution fusion | flops 5640814592 | bytes 13893632 | tf_op jit(solution)/shard_map/dot_general | solution.py:22
  18.5 66.1 %all-reduce.5.cloned.1.call-done = f32[1792,256]{1,0:T(8,128)} async-done(((f32[1792,256]{1,0:T(8,128)}), f32[1792,256]{1,0:T(8,128)}) %all-reduce.5.cloned.1.call-update) | async-done | bytes 1835024 | tf_op jit(solution)/shard_map/psum | solution.py:23
  84.6 5.9 %fusion.14 = f32[256,256]{0,1:T(8,128)} fusion(f32[1792,256]{1,0:T(8,128)} %all-reduce.5.cloned.1.call-done), kind=kOutput, calls=%fused_computation.40 | convolution fusion | flops 1409286144 | bytes 2097152 | tf_op jit(solution)/shard_map/dot_general | solution.py:15
  90.9 84.4 %all-reduce.7.cloned.1.call-done = f32[256,256]{0,1:T(8,128)} async-done(((f32[256,256]{0,1:T(8,128)}), f32[256,256]{0,1:T(8,128)}) %all-reduce.7.cloned.1.call-update) | async-done | bytes 262160 | tf_op jit(solution)/shard_map/psum | solution.py:24
  175.3 1.1 copy.7
  176.4 1.0 fusion.4
  178.1 11.7 %cholesky.50 = f32[128,128]{1,0:T(8,128)S(1)} custom-call(f32[128,128]{1,0:T(8,128)S(1)} %cholesky.118), custom_call_target="Cholesky" | custom-call | tf_op jit(solution)/shard_map/jit(cholesky)/cholesky | solution.py:25
  189.9 9.8 %custom-call.14 = f32[1,128,128]{1,2,0:T(8,128)S(1)} custom-call(f32[1,128,128]{2,1,0:T(8,128)S(1)} %get-tuple-element.24), custom_call_target="InvertDiagBlocksLowerTriangular" | custom-call | tf_op jit(solution)/shard_map/jit(cholesky)/cholesky | solution.py:25
  199.7 1.0 constant_dynamic-update-slice_fusion.1
  200.7 1.1 convolution_subtract_fusion.1
  201.8 11.7 %cholesky.105 = f32[128,128]{1,0:T(8,128)S(1)} custom-call(f32[128,128]{1,0:T(8,128)S(1)} %convolution_subtract_fusion.1), custom_call_target="Cholesky" | custom-call | tf_op jit(solution)/shard_map/jit(cholesky)/cholesky | solution.py:25
  215.6 4.5 %while.1 = (s32[]{:T(128)}, f32[256,256]{1,0:T(8,128)S(1)}, s32[2,2]{1,0:T(2,128)S(1)}, f32[2,128,128]{2,1,0:T(8,128)S(1)}, s32[]{:T(128)}) while((s32[]{:T(128)}, f32[256,256]{1,0:T(8,128)S(1)}, s32[2,2]{1,0:T(2,128)S(1)}, f32[2,128,128]{2,1,0:T(8,128)S(1)}, s32[]{:T(128)}) %tuple.27), condition=%wide.while_cond, body=%wide.while_body.sunk | while | flops 2 | bytes 131189 | solution.py:26
  216.8 1.4 bitcast_dynamic-update-slice_fusion.2
  218.8 1.4 bitcast_dynamic-update-slice_fusion.2
  220.2 19.7 %custom-call.15 = f32[2,128,128]{1,2,0:T(8,128)S(1)} custom-call(f32[2,128,128]{2,1,0:T(8,128)S(1)} %get-tuple-element.10), custom_call_target="InvertDiagBlocksLowerTriangular" | custom-call | tf_op jit(solution)/shard_map/triangular_solve | solution.py:26
  240.8 1.6 convolution_subtract_fusion
  243.4 14.7 %fusion = f32[1024,256]{1,0:T(8,128)} fusion(f32[1792,1024]{1,0:T(8,128)} %param.4, bf16[1792,1024]{1,0:T(8,128)(2,1)S(1)} %copy-done.1, f32[1792,128]{0,1:T(8,128)S(1)} %fusion.5, f32[1792,128]{0,1:T(8,128)S(1)} %fusion.2), kind=kOutput, calls=%fused_computation.5 | convolution fusion | flops 5641273344 | bytes 13893632 | tf_op jit(solution)/shard_map/dot_general | solution.py:15
  258.2 86.4 %all-reduce.9.cloned.1.call-done = f32[1024,256]{1,0:T(8,128)} async-done(((f32[1024,256]{1,0:T(8,128)}), f32[1024,256]{1,0:T(8,128)}) %all-reduce.9.cloned.1.call-update) | async-done | bytes 1048592 | tf_op jit(solution)/shard_map/psum | solution.py:29
  344.6 1.4 multiply_reduce_fusion
  346.0 14.0 %psum.31 = f32[256]{0:T(256)S(1)} all-reduce(f32[256]{0:T(256)S(1)} %multiply_reduce_fusion), channel_id=1, replica_groups=mesh['fsdp'=16,'tp'=8] {'tp'}, use_global_device_ids=true, to_apply=%region_8.9 | all-reduce | flops 256 | bytes 2048 | tf_op jit(solution)/shard_map/psum | solution.py:33
  360.0 1.3 broadcast_multiply_fusion
  361.3 13.3 %multiply_convert_fusion = bf16[1792,1024]{1,0:T(8,128)(2,1)} fusion(f32[1024,256]{1,0:T(8,128)S(1)} %broadcast_multiply_fusion, f32[1792,128]{0,1:T(8,128)S(1)} %fusion.5, f32[1792,128]{0,1:T(8,128)S(1)} %copy-done.5), kind=kOutput, calls=%fused_computation.2 | convolution fusion | flops 5641273344 | bytes 6553600 | tf_op jit(solution)/shard_map/dot_general | solution.py:37
  374.7 16.6 %multiply_subtract_fusion = f32[1792,1024]{1,0:T(8,128)} fusion(f32[1024,256]{1,0:T(8,128)S(1)} %copy-done.6, f32[1792,1024]{1,0:T(8,128)} %param.4, bf16[1792,1024]{1,0:T(8,128)(2,1)S(1)} %copy-done.2, f32[1792,128]{0,1:T(8,128)S(1)} %fusion.5, f32[1792,128]{0,1:T(8,128)S(1)} %copy-done.5), kind=kOutput, calls=%fused_computation.3 | convolution fusion | flops 5644943360 | bytes 21233664 | tf_op jit(solution)/shard_map/dot_general | solution.py:30
  (39 shorter events, 5.1 us)
Async XLA Ops:
  7.2 1.2 copy-start
  7.2 77.4 %all-reduce.5.cloned.1.call-start = ((), (), s32[]{:S(2)}) async-start(), calls=%async_computation | async-start | bytes 3670016 | tf_op jit(solution)/shard_map/psum | solution.py:23
  18.4 156.9 %all-reduce.7.cloned.1.call-start = ((), (), s32[]{:S(2)}) async-start(), calls=%async_computation.1 | async-start | bytes 524288 | tf_op jit(solution)/shard_map/psum | solution.py:24
  84.6 155.2 %copy-start.3 = (f32[1792,256]{1,0:T(8,128)S(1)}, f32[1792,256]{1,0:T(8,128)}, u32[]{:S(2)}) copy-start(f32[1792,256]{1,0:T(8,128)} %all-reduce.5.cloned.1.call-done) | copy-start | bytes 5505028
  90.6 254.0 %all-reduce.9.cloned.1.call-start = ((), (), s32[]{:S(2)}) async-start(), calls=%async_computation.2 | async-start | bytes 2097152 | tf_op jit(solution)/shard_map/psum | solution.py:29
  177.4 0.7 copy-start.8
  239.8 3.6 copy-start.1
  240.8 2.6 copy-start.4
  258.2 103.1 %copy-start.5 = (f32[1792,128]{0,1:T(8,128)S(1)}, f32[1792,128]{0,1:T(8,128)}, u32[]{:S(2)}) copy-start(f32[1792,128]{0,1:T(8,128)} %copy-done.4) | copy-start | bytes 2752516
  361.3 13.4 %copy-start.7 = (f32[1024,256]{1,0:T(8,128)}, f32[1024,256]{1,0:T(8,128)S(1)}, u32[]{:S(2)}) copy-start(f32[1024,256]{1,0:T(8,128)S(1)} %broadcast_multiply_fusion) | copy-start | bytes 3145732
  361.3 13.4 %copy-start.2 = (bf16[1792,1024]{1,0:T(8,128)(2,1)S(1)}, bf16[1792,1024]{1,0:T(8,128)(2,1)}, u32[]{:S(2)}) copy-start(bf16[1792,1024]{1,0:T(8,128)(2,1)} %param.3) | copy-start | bytes 11010052
  361.3 13.4 %copy-start.6 = (f32[1024,256]{1,0:T(8,128)S(1)}, f32[1024,256]{1,0:T(8,128)}, u32[]{:S(2)}) copy-start(f32[1024,256]{1,0:T(8,128)} %all-reduce.9.cloned.1.call-done) | copy-start | bytes 3145732
Sparse Core Ops, SparseCore 0:
  18.5 66.0 all-reduce.4
  90.7 84.5 all-reduce.6
  258.3 86.2 all-reduce.8
where the time goes:
time: 403 us; the launch traced here: 398 us
  waiting for transfers between devices  237 us (59%)
  matrix products  66.3 us (16%)
  other arithmetic  57.3 us (14%)
  between operations  15.5 us (4%)
  blocking collectives  14 us (3%)
  local copies, waits for them, and re-layouts  7.03 us (2%)
    psum x1, waiting for transfers between devices, body(): back = lax.psum(transposed(blend, ortho), 'fsdp')  86.4 us
    psum x1, waiting for transfers between devices, body(): gram = lax.psum(transposed(projected, projected), 'fsdp')  84.4 us
    psum x1, waiting for transfers between devices, body(): projected = lax.psum(partial_proj, 'tp')  66.1 us
    another operation x6, other arithmetic, body(): factor = jnp.linalg.cholesky(gram)  33.9 us
    dot_general x2, matrix products, transposed(): lax.dot_general(left, right, (((0,), (0,)), ((), ())), precision=HIGH, pr...  20.7 us
    another operation x3, other arithmetic, body(): lax.linalg.triangular_solve(factor, projected, left_side=False, lower=Tru...  19.7 us
    dot_general x1, matrix products, body(): jnp.dot(ortho, back.T, precision=HIGH, preferred_element_type=jnp.float32)  16.6 us
    psum x1, blocking collectives, body(): squares = lax.psum(jnp.sum(back * back, axis=0), 'tp')  14 us
  transfers between devices with their start and end apart: 3, of which 3 were waited for; matrix products, arithmetic and copies ran while one was open for 0% of the time, Pallas kernels for 0%

commit v1 on v0

v1 whole, which is shorter than its diff:
```python
import functools

import jax
import jax.numpy as jnp
from jax import lax
from jax.experimental import pallas as pl
from jax.experimental.pallas import tpu as pltpu
from jax.sharding import PartitionSpec as P

ROWS = 28672
COLS = 8192
RANK = 256

F32 = jnp.float32
BF16 = jnp.bfloat16
HIGH = lax.Precision.HIGHEST
MESH = pl.DeviceIdType.MESH

LOCAL_ROWS = 1792
LOCAL_COLS = 1024
HALF = 896
PIECE = 224
PART = 112
WIDE = 512


class Names:
    def __init__(self):
        self.count = 0

    def take(self, many=1):
        first = self.count
        self.count += many
        return first


NAMES = Names()
N_HOP_A, N_HOP_B = NAMES.take(), NAMES.take()
N_LEFT_A, N_LEFT_B = NAMES.take(), NAMES.take()
N_RIGHT_A, N_RIGHT_B = NAMES.take(), NAMES.take()
G_LEFT_A, G_LEFT_B = NAMES.take(), NAMES.take()
G_RIGHT_A, G_RIGHT_B = NAMES.take(), NAMES.take()
G_OPP_A, G_OPP_B = NAMES.take(), NAMES.take()
N_CORE = NAMES.take(4)
G_CORE = NAMES.take(4)
GRAM_SUM = NAMES.take(15)
GRAM_X = NAMES.take(3)
GRAM_ALL = NAMES.take(15)
SQ = NAMES.take(7)
GRAM_CORE = NAMES.take()
W_HOP = NAMES.take(4)
W_NEXT = NAMES.take(8)
W_RING = NAMES.take(8)
W_FAR = NAMES.take(4)
W_SUB = NAMES.take(6)
W_ALL = NAMES.take(6)


def nn(a, b, precision=None):
    return lax.dot_general(
        a, b, (((1,), (0,)), ((), ())), precision=precision, preferred_element_type=F32
    )


def tn(a, b, precision=None):
    return lax.dot_general(
        a, b, (((0,), (0,)), ((), ())), precision=precision, preferred_element_type=F32
    )


def nt(a, b, precision=None):
    return lax.dot_general(
        a, b, (((1,), (1,)), ((), ())), precision=precision, preferred_element_type=F32
    )


def pick(index, values):
    out = values[0]
    for at in range(1, len(values)):
        out = out + (values[at] - values[at - 1]) * ((index + len(values) - at) // len(values))
    return out


def split(x):
    hi = x.astype(BF16)
    return hi, (x - hi.astype(F32)).astype(BF16)


def row_copy(x, j):
    return jnp.broadcast_to(x[j : j + 1, :], (8, 128))


def inverse_factor(x):
    n = len(x)
    sub = lax.broadcasted_iota(jnp.int32, (8, 128), 0)
    lane = lax.broadcasted_iota(jnp.int32, (8, 128), 1)
    col = [
        [None if i < k // 8 else jnp.broadcast_to(x[i][:, k : k + 1], (8, 128)) for i in range(n)]
        for k in range(8 * n)
    ]
    inverse = [jnp.where(lane == sub + 8 * i, 1.0, 0.0) for i in range(n)]
    for j in range(8 * n):
        g, r = j // 8, j % 8
        pivot = row_copy(col[j][g], r)
        inv = 1.0 / pivot
        row = row_copy(inverse[g], r)
        entry = {k: row_copy(col[j][k // 8], k % 8) for k in range(j + 1, 8 * n)}
        mult = [None if i < g else col[j][i] * inv for i in range(n)]
        if r < 7:
            mult[g] = jnp.where(sub > r, mult[g], 0.0)
        for k in range(j + 1, 8 * n):
            for i in range(k // 8, n):
                col[k][i] = col[k][i] - mult[i] * entry[k]
        for i in range(g + (r == 7), n):
            inverse[i] = inverse[i] - mult[i] * row
        inverse[g] = jnp.where(sub == r, row * lax.rsqrt(pivot), inverse[g])
    return jnp.concatenate(inverse, axis=0)


def eliminate(k, m_ref):
    rows = pl.ds(pl.multiple_of(32 * k, 32), 32)
    tile = pl.ds(pl.multiple_of(128 * (k // 4), 128), 128)
    d = pltpu.roll(m_ref[rows, tile], (128 - 32 * (k % 4)) % 128, 1)
    inverse = inverse_factor([d[8 * i : 8 * i + 8] for i in range(4)])
    scaled = nn(inverse[:, :32], m_ref[rows, :], HIGH)
    m_ref[rows, :] = scaled

    @pl.when(k < 7)
    def _():
        subl = lax.broadcasted_iota(jnp.int32, (RANK, 32), 0)
        lower = jnp.where(subl >= 32 * k + 32, scaled[:, :RANK].T, 0.0)
        m_ref[...] -= nn(lower, scaled, HIGH)


def main_kernel(
    grad,
    mom,
    basis,
    blend_out,
    ortho_out,
    back_out,
    norm_out,
    grad_v,
    basis_v,
    bases,
    hi_v,
    lo_v,
    part_v,
    from_core,
    hop_v,
    side_v,
    proj,
    gram_part,
    gram_in,
    gram_x,
    gram,
    elim,
    turned,
    w,
    w_hop,
    w_side,
    w_sub,
    w_full,
    sq_v,
    load_sem,
    send_sem,
    recv_sem,
):
    f = lax.axis_index("fsdp")
    t = lax.axis_index("tp")
    x, c = t // 2, t % 2
    z, y = f // 4, f % 4

    def tp_dev(xx, cc):
        return {"fsdp": f, "tp": xx * 2 + cc}

    def f_dev(ff):
        return {"fsdp": ff, "tp": t}

    right = tp_dev((x + 1) % 4, c)
    left = tp_dev((x + 3) % 4, c)
    twin = tp_dev(x, 1 - c)

    def remote(src, dst, number, device):
        return pltpu.make_async_remote_copy(
            src_ref=src,
            dst_ref=dst,
            send_sem=send_sem.at[number],
            recv_sem=recv_sem.at[number],
            device_id=device,
            device_id_type=MESH,
        )

    def send(src, dst, number, device):
        remote(src, dst, number, device).start()

    def arrive(dst, number):
        remote(dst, dst, number, twin).wait_recv()

    def all_sent(first, many, ref):
        @pl.loop(first, first + many)
        def _(number):
            remote(ref, ref, number, twin).wait_send()

    def piece_row(core, chip):
        return pl.multiple_of(core * HALF + chip * PIECE, 32)

    def chunk_row(i):
        g = 3 - i // 2
        d = g + (g // 2) * (1 - 2 * (g % 2))
        core = (1 - c) * (1 - i % 2) + c * (i % 2)
        return piece_row(core, (x + d) % 4)

    def load(i):
        rows = pl.ds(chunk_row(i), PIECE)
        return (
            pltpu.make_async_copy(mom.at[rows], blend_out.at[rows], load_sem.at[2 * i]),
            pltpu.make_async_copy(grad.at[rows], grad_v.at[i % 4], load_sem.at[2 * i + 1]),
        )

    basis_copy = pltpu.make_async_copy(basis, basis_v, load_sem.at[16])
    basis_copy.start()

    @pl.loop(0, 3)
    def _(i):
        for copy in load(i):
            copy.start()

    barrier = pltpu.get_barrier_semaphore()

    @pl.loop(1, 16)
    def _(d):
        pl.semaphore_signal(barrier, inc=1, device_id=f_dev((f + d) % 16), device_id_type=MESH)

    @pl.loop(1, 8)
    def _(d):
        pl.semaphore_signal(
            barrier, inc=1, device_id={"fsdp": f, "tp": (t + d) % 8}, device_id_type=MESH
        )

    basis_copy.wait()
    basis_hi, basis_lo = split(basis_v[...])
    bases[:LOCAL_COLS] = basis_hi
    bases[LOCAL_COLS : 2 * LOCAL_COLS] = basis_lo
    bases[2 * LOCAL_COLS :] = basis_hi
    turned[...] = jnp.zeros_like(turned)
    hi_v[LOCAL_ROWS:, :] = jnp.zeros((32, LOCAL_COLS), BF16)
    lo_v[LOCAL_ROWS:, :] = jnp.zeros((32, LOCAL_COLS), BF16)

    def partial(i):
        for copy in load(i):
            copy.wait()
        rows = pl.ds(chunk_row(i), PIECE)

        @pl.when(i < 5)
        def _():
            for copy in load(i + 3):
                copy.start()

        blend = blend_out[rows, :] + grad_v[i % 4].astype(F32)
        blend_out[rows, :] = blend
        hi, lo = split(blend)
        hi_v[rows, :] = hi
        lo_v[rows, :] = lo
        return nn(jnp.concatenate([hi, hi, lo], axis=1), bases[...])

    a_rows, b_rows = pl.ds(0, PART), pl.ds(PART, PART)

    def add_core(j):
        arrive(from_core.at[j], N_CORE + j)
        part_v[2 * j + 1] += from_core[j]

    @pl.loop(0, 8)
    def _(i):
        part_v[i] = partial(i)
        j = i // 2
        core = remote(part_v.at[i], from_core.at[j], N_CORE + j, twin)

        @pl.when(i == 0)
        def _():
            pl.semaphore_wait(barrier, 22)

        @pl.when(i % 2 == 0)
        def _():
            core.start()

        @pl.when(i == 2)
        def _():
            add_core(0)
            send(part_v.at[1, a_rows], hop_v.at[0], N_HOP_A, right)
            send(part_v.at[1, b_rows], hop_v.at[1], N_HOP_B, left)

        @pl.when(i == 4)
        def _():
            add_core(1)
            send(part_v.at[3, a_rows], side_v.at[2], N_RIGHT_A, left)

        @pl.when(i == 6)
        def _():
            add_core(2)
            send(part_v.at[5, b_rows], side_v.at[1], N_LEFT_B, right)

    add_core(3)
    arrive(hop_v.at[0], N_HOP_A)
    part_v[5, a_rows] += hop_v[0]
    send(part_v.at[5, a_rows], side_v.at[0], N_LEFT_A, right)
    arrive(hop_v.at[1], N_HOP_B)
    part_v[3, b_rows] += hop_v[1]
    send(part_v.at[3, b_rows], side_v.at[3], N_RIGHT_B, left)

    my_row = piece_row(c, x)
    arrive(side_v.at[2], N_RIGHT_A)
    arrive(side_v.at[0], N_LEFT_A)
    proj[pl.ds(my_row, PART), :] = part_v[7, a_rows] + (side_v[0] + side_v[2])
    arrive(side_v.at[1], N_LEFT_B)
    arrive(side_v.at[3], N_RIGHT_B)
    proj[pl.ds(my_row + PART, PART), :] = part_v[7, b_rows] + (side_v[1] + side_v[3])

    def part_of(core, chip, b):
        return proj.at[pl.ds(pl.multiple_of(piece_row(core, chip) + b * PART, 16), PART)]

    def whole_of(core, chip):
        return proj.at[pl.ds(piece_row(core, chip), PIECE)]

    def send_part(chip, b, number, device):
        send(part_of(c, chip, b), part_of(c, chip, b), number, device)

    def send_whole(chip, number):
        send(whole_of(c, chip), whole_of(c, chip), number, twin)

    xl, xr, xo = (x + 3) % 4, (x + 1) % 4, (x + 2) % 4
    send_part(x, 0, G_LEFT_A, right)
    send_part(x, 1, G_RIGHT_B, left)
    send_whole(x, G_CORE)
    send_part(x, 1, G_LEFT_B, right)
    send_part(x, 0, G_RIGHT_A, left)

    half_cols = pl.ds(pl.multiple_of(c * 128, 128), 128)

    def eight(row):
        return pl.ds(pl.multiple_of(row * 8, 8), 8)

    def gram_start():
        gram_part[...] = jnp.zeros((128, RANK), F32)

        @pl.loop(0, 2)
        def _(core):
            rows = pl.ds(piece_row(core, x), PIECE)
            gram_part[...] += tn(proj[rows, half_cols], proj[rows, :], HIGH)

        @pl.loop(1, 16)
        def _(d):
            to = (f + d) % 16
            send(gram_part.at[eight(to)], gram_in.at[d], GRAM_SUM + d - 1, f_dev(to))

    def gram_across():
        gram_in[0] = gram_part[eight(f), :]

        @pl.loop(1, 16)
        def _(d):
            arrive(gram_in.at[d], GRAM_SUM + d - 1)

        gram_x[x] = jnp.sum(gram_in[...], axis=0)

        @pl.loop(1, 4)
        def _(d):
            send(gram_x.at[x], gram_x.at[x], GRAM_X + d - 1, tp_dev((x + d) % 4, c))

    def gram_row(ff):
        return pl.ds(pl.multiple_of(c * 128 + ff * 8, 8), 8)

    def gram_round():
        @pl.loop(1, 4)
        def _(d):
            arrive(gram_x.at[(x + 4 - d) % 4], GRAM_X + d - 1)

        gram[gram_row(f), :] = (gram_x[0] + gram_x[1]) + (gram_x[2] + gram_x[3])

        @pl.loop(1, 16)
        def _(d):
            mine = gram.at[gram_row(f)]
            send(mine, mine, GRAM_ALL + d - 1, f_dev((f + d) % 16))

    def gram_half(core):
        return gram.at[pl.ds(pl.multiple_of(core * 128, 128), 128)]

    def gram_pair():
        @pl.loop(1, 16)
        def _(d):
            arrive(gram.at[gram_row((f + 16 - d) % 16)], GRAM_ALL + d - 1)

        send(gram_half(c), gram_half(c), GRAM_CORE, twin)

    w[...] = jnp.zeros_like(w)

    @pl.loop(0, 8)
    def _(g):
        core = (c + pick(g, (0, 1, 0, 0, 0, 1, 1, 1))) % 2
        chip = (x + pick(g, (0, 0, 1, 3, 2, 1, 3, 2))) % 4

        @pl.when(g == 1)
        def _():
            arrive(whole_of(1 - c, x), G_CORE)
            gram_start()

        @pl.when(g == 2)
        def _():
            arrive(part_of(c, xl, 0), G_LEFT_A)
            send_part(xl, 0, G_OPP_A, right)
            arrive(part_of(c, xr, 1), G_RIGHT_B)
            send_part(xr, 1, G_OPP_B, left)
            gram_across()
            arrive(part_of(c, xr, 0), G_RIGHT_A)
            send_whole(xr, G_CORE + 1)
            arrive(part_of(c, xl, 1), G_LEFT_B)
            send_whole(xl, G_CORE + 2)

        @pl.when(g == 4)
        def _():
            arrive(part_of(c, xo, 0), G_OPP_A)
            arrive(part_of(c, xo, 1), G_OPP_B)
            send_whole(xo, G_CORE + 3)
            gram_round()

        @pl.when(g == 5)
        def _():
            arrive(whole_of(1 - c, xr), G_CORE + 1)

        @pl.when(g == 6)
        def _():
            arrive(whole_of(1 - c, xl), G_CORE + 2)

        @pl.when(g == 7)
        def _():
            arrive(whole_of(1 - c, xo), G_CORE + 3)

        rows = pl.ds(piece_row(core, chip), PIECE)
        p_hi, p_lo = split(proj[rows, :].T)
        turned[:, :PIECE] = p_hi
        turned[:, 256 : 256 + PIECE] = p_hi
        turned[:, 512 : 512 + PIECE] = p_lo
        more = pl.ds(piece_row(core, chip), 256)
        for n in range(4):
            cols = slice(256 * n, 256 * n + 256)
            hi = hi_v[more, cols]
            w[:, cols] += nn(turned[...], jnp.concatenate([hi, lo_v[more, cols], hi], axis=0))

    def places(h):
        k, q = y + h * (z - y), z + h * (y - z)

        def first(kk):
            return f_dev(z * 4 + kk + h * (kk * 4 + y - z * 4 - kk))

        def second(qq):
            return f_dev(qq * 4 + y + h * (z * 4 + qq - qq * 4 - y))

        return k, q, first, second

    ca, cb = pl.ds(0, WIDE), pl.ds(WIDE, WIDE)

    def rows32(h, k):
        return pl.ds(pl.multiple_of(128 * h + 32 * k, 32), 32)

    def rows8(h, k, q):
        return pl.ds(pl.multiple_of(128 * h + 32 * k + 8 * q, 8), 8)

    def w_step_1(h):
        k, q, first, _ = places(h)
        kr, kl, ko = (k + 1) % 4, (k + 3) % 4, (k + 2) % 4
        send(w.at[rows32(h, ko), ca], w_hop.at[2 * h], W_HOP + 2 * h, first(kr))
        send(w.at[rows32(h, ko), cb], w_hop.at[2 * h + 1], W_HOP + 2 * h + 1, first(kl))
        send(w.at[rows32(h, kr), cb], w_side.at[4 * h + 1], W_NEXT + 4 * h + 1, first(kr))
        send(w.at[rows32(h, kl), ca], w_side.at[4 * h + 2], W_NEXT + 4 * h + 2, first(kl))

    def w_step_2(h):
        k, q, first, _ = places(h)
        kr, kl = (k + 1) % 4, (k + 3) % 4
        arrive(w_hop.at[2 * h], W_HOP + 2 * h)
        w[rows32(h, kr), ca] += w_hop[2 * h]
        send(w.at[rows32(h, kr), ca], w_side.at[4 * h], W_NEXT + 4 * h, first(kr))
        arrive(w_hop.at[2 * h + 1], W_HOP + 2 * h + 1)
        w[rows32(h, kl), cb] += w_hop[2 * h + 1]
        send(w.at[rows32(h, kl), cb], w_side.at[4 * h + 3], W_NEXT + 4 * h + 3, first(kl))

    def w_step_3(h):
        k, q, _, second = places(h)
        for s in range(4):
            arrive(w_side.at[4 * h + s], W_NEXT + 4 * h + s)
        w[rows32(h, k), ca] += w_side[4 * h] + w_side[4 * h + 2]
        w[rows32(h, k), cb] += w_side[4 * h + 1] + w_side[4 * h + 3]

        @pl.loop(1, 4)
        def _(d):
            to, slot = (q + d) % 4, 3 * h + d - 1
            send(w.at[rows8(h, k, to)], w_sub.at[slot], W_SUB + slot, second(to))

    def w_step_4(h):
        k, q, _, second = places(h)

        @pl.loop(0, 3)
        def _(d):
            arrive(w_sub.at[3 * h + d], W_SUB + 3 * h + d)

        w_full[rows8(h, k, q), :] = (w[rows8(h, k, q), :] + w_sub[3 * h]) + (
            w_sub[3 * h + 1] + w_sub[3 * h + 2]
        )

        @pl.loop(1, 4)
        def _(d):
            mine = w_full.at[rows8(h, k, q)]
            send(mine, mine, W_ALL + 3 * h + d - 1, second((q + d) % 4))

    def w_step_5(h):
        k, q, first, _ = places(h)
        dr, dl = first((k + 1) % 4), first((k + 3) % 4)

        @pl.loop(1, 4)
        def _(d):
            arrive(w_full.at[rows8(h, k, (q + 4 - d) % 4)], W_ALL + 3 * h + d - 1)

        mine_a, mine_b = w_full.at[rows32(h, k), ca], w_full.at[rows32(h, k), cb]
        send(mine_a, mine_a, W_RING + 4 * h, dr)
        send(mine_b, mine_b, W_RING + 4 * h + 3, dl)
        send(mine_b, mine_b, W_RING + 4 * h + 1, dr)
        send(mine_a, mine_a, W_RING + 4 * h + 2, dl)

    def w_step_6(h):
        k, q, first, _ = places(h)
        kr, kl = (k + 1) % 4, (k + 3) % 4
        from_left = w_full.at[rows32(h, kl), ca]
        arrive(from_left, W_RING + 4 * h)
        send(from_left, from_left, W_FAR + 2 * h, first(kr))
        from_right = w_full.at[rows32(h, kr), cb]
        arrive(from_right, W_RING + 4 * h + 3)
        send(from_right, from_right, W_FAR + 2 * h + 1, first(kl))

    def w_step_7(h):
        k = places(h)[0]
        kr, kl, ko = (k + 1) % 4, (k + 3) % 4, (k + 2) % 4
        arrive(w_full.at[rows32(h, kl), cb], W_RING + 4 * h + 1)
        arrive(w_full.at[rows32(h, kr), ca], W_RING + 4 * h + 2)
        arrive(w_full.at[rows32(h, ko), ca], W_FAR + 2 * h)
        arrive(w_full.at[rows32(h, ko), cb], W_FAR + 2 * h + 1)

    def both_halves(step):
        @pl.loop(0, 2)
        def _(h):
            step(h)

    both_halves(w_step_1)
    gram_pair()
    w_steps_at = (w_step_2, None, w_step_3, w_step_4, None, w_step_5, w_step_6, w_step_7)

    arrive(gram_half(1 - c), GRAM_CORE)
    elim[:, :RANK] = gram[...]
    rr = lax.broadcasted_iota(jnp.int32, (RANK, RANK), 0)
    cc = lax.broadcasted_iota(jnp.int32, (RANK, RANK), 1)
    elim[:, RANK:] = jnp.where(rr == cc, 1.0, 0.0).astype(F32)

    @pl.loop(0, 8)
    def _(k):
        eliminate(k, elim)
        for at, step in enumerate(w_steps_at):
            if step is not None:

                @pl.when(k == at)
                def _():
                    both_halves(step)

    f_hi, f_lo = split(elim[:, RANK:])
    factor = jnp.concatenate([f_hi, f_hi, f_lo], axis=1)
    squares = jnp.zeros((RANK, 128), F32)
    for n in range(4):
        cols = slice(256 * n, 256 * n + 256)
        w_hi, w_lo = split(w_full[:, cols])
        back = nn(factor, jnp.concatenate([w_hi, w_lo, w_hi], axis=0))
        back_out[:, cols] = back
        squares = squares + (back[:, :128] * back[:, :128] + back[:, 128:] * back[:, 128:])
    sq_v[t] = nt(jnp.ones((8, 128), F32), squares, HIGH)

    @pl.loop(1, 8)
    def _(d):
        send(sq_v.at[t], sq_v.at[t], SQ + d - 1, {"fsdp": f, "tp": (t + d) % 8})


    t_hi, t_lo = split(elim[:, RANK:].T)
    turned[:, :256] = t_hi
    turned[:, 256:512] = t_lo

    @pl.loop(0, 8)
    def _(i):
        rows = pl.ds(pl.multiple_of(i * PIECE, 32), PIECE)
        hi, lo = split(proj[rows, :])
        first = turned[:, :256]
        ortho_out[rows, :] = nn(
            jnp.concatenate([hi, hi, lo], axis=1),
            jnp.concatenate([first, turned[:, 256:512], first], axis=0),
        )

    all_sent(N_HOP_A, 12, side_v.at[0])
    all_sent(N_CORE, 8, part_v.at[0])
    all_sent(GRAM_SUM, 33, sq_v.at[0])
    all_sent(GRAM_CORE, 1, gram_part)
    all_sent(W_HOP, 24, w_hop.at[0])
    all_sent(W_SUB, 12, w_sub.at[0])

    @pl.loop(1, 8)
    def _(d):
        arrive(sq_v.at[(t + 8 - d) % 8], SQ + d - 1)

    norm_out[...] = lax.rsqrt(jnp.sum(sq_v[...], axis=0) + 1e-06)
    all_sent(SQ, 7, sq_v.at[0])


def write_kernel(
    blend, ortho, back, norm, mom_out, basis_out, update_out, backs, mom_v, basis_v, update_v, sems
):
    hi, lo = split(back[...])
    backs[:RANK] = hi
    backs[RANK : 2 * RANK] = lo
    backs[2 * RANK :] = hi
    scale = (ROWS * COLS / RANK) ** 0.5
    norms = norm[0:1, :]

    def copies(i):
        rows = pl.ds(pl.multiple_of(i * PIECE, 32), PIECE)
        rank_rows = pl.ds(pl.multiple_of(i * 128, 128), 128)
        slot = i % 2
        return (
            pltpu.make_async_copy(mom_v.at[slot], mom_out.at[rows], sems.at[slot, 0]),
            pltpu.make_async_copy(update_v.at[slot], update_out.at[rows], sems.at[slot, 1]),
            pltpu.make_async_copy(basis_v.at[slot], basis_out.at[rank_rows], sems.at[slot, 2]),
        )

    @pl.loop(0, 8)
    def _(i):
        slot = i % 2

        @pl.when(i >= 2)
        def _():
            for copy in copies(i - 2):
                copy.wait()

        rows = pl.ds(pl.multiple_of(i * PIECE, 32), PIECE)
        cols = pl.ds(pl.multiple_of(i * 128, 128), 128)
        basis_v[slot] = back[:, cols].T * norms
        plain = ortho[rows, :]
        mom_v[slot] = blend[rows, :] - nn((0.05 * plain).astype(BF16), backs[:RANK])
        hi, lo = split(plain * (scale * norms))
        update_v[slot] = nn(jnp.concatenate([hi, hi, lo], axis=1), backs[...]).astype(BF16)
        for copy in copies(i):
            copy.start()

    for i in (6, 7):
        for copy in copies(i):
            copy.wait()


def body(gradient, momentum, basis):
    anywhere = pl.BlockSpec(memory_space=pl.ANY)
    inside = pl.BlockSpec(memory_space=pltpu.VMEM)
    vmem = pltpu.VMEM
    fixed = [pltpu.with_memory_space_constraint(a, pltpu.HBM) for a in (gradient, momentum, basis)]
    results = pl.pallas_call(
        main_kernel,
        out_shape=(
            vmem((LOCAL_ROWS, LOCAL_COLS), F32),
            vmem((LOCAL_ROWS, RANK), F32),
            vmem((RANK, LOCAL_COLS), F32),
            vmem((8, RANK), F32),
        ),
        in_specs=[anywhere] * 3,
        out_specs=(inside,) * 4,
        scratch_shapes=[
            vmem((4, PIECE, LOCAL_COLS), BF16),
            vmem((LOCAL_COLS, RANK), F32),
            vmem((3 * LOCAL_COLS, RANK), BF16),
            vmem((LOCAL_ROWS + 32, LOCAL_COLS), BF16),
            vmem((LOCAL_ROWS + 32, LOCAL_COLS), BF16),
            vmem((8, PIECE, RANK), F32),
            vmem((4, PIECE, RANK), F32),
            vmem((2, PART, RANK), F32),
            vmem((4, PART, RANK), F32),
            vmem((LOCAL_ROWS, RANK), F32),
            vmem((128, RANK), F32),
            vmem((16, 8, RANK), F32),
            vmem((4, 8, RANK), F32),
            vmem((RANK, RANK), F32),
            vmem((RANK, 2 * RANK), F32),
            vmem((RANK, 3 * 256), BF16),
            vmem((RANK, LOCAL_COLS), F32),
            vmem((4, 32, WIDE), F32),
            vmem((8, 32, WIDE), F32),
            vmem((6, 8, LOCAL_COLS), F32),
            vmem((RANK, LOCAL_COLS), F32),
            vmem((8, 8, RANK), F32),
            pltpu.SemaphoreType.DMA((17,)),
            pltpu.SemaphoreType.DMA((NAMES.count,)),
            pltpu.SemaphoreType.DMA((NAMES.count,)),
        ],
        compiler_params=pltpu.CompilerParams(
            collective_id=0, has_side_effects=True, vmem_limit_bytes=44 * 2**20
        ),
        name="transfers",
    )(*fixed)
    results = [pltpu.with_memory_space_constraint(a, pltpu.VMEM) for a in results]

    return pl.pallas_call(
        write_kernel,
        out_shape=(
            jax.ShapeDtypeStruct((LOCAL_ROWS, LOCAL_COLS), F32),
            jax.ShapeDtypeStruct((LOCAL_COLS, RANK), F32),
            jax.ShapeDtypeStruct((LOCAL_ROWS, LOCAL_COLS), BF16),
        ),
        in_specs=[inside] * 4,
        out_specs=(anywhere,) * 3,
        scratch_shapes=[
            vmem((3 * RANK, LOCAL_COLS), BF16),
            vmem((2, PIECE, LOCAL_COLS), F32),
            vmem((2, 128, RANK), F32),
            vmem((2, PIECE, LOCAL_COLS), BF16),
            pltpu.SemaphoreType.DMA((2, 3)),
        ],
        compiler_params=pltpu.CompilerParams(vmem_limit_bytes=32 * 2**20),
        name="outputs",
    )(*results)


def solution(mesh):
    placed = (P("fsdp", "tp"), P("fsdp", "tp"), P("tp", None))
    return jax.shard_map(
        body,
        mesh=mesh,
        in_specs=placed,
        out_specs=(P("fsdp", "tp"), P("tp", None), P("fsdp", "tp")),
        check_vma=False,
    )
```

time: 403 us -> 72.2 us (0.18); the launches traced: 398 us -> 72.1 us
  waiting for transfers between devices: 237 us -> 0 us
  Pallas kernels: 0 us -> 71.5 us
  matrix products: 66.3 us -> 0 us
  other arithmetic: 57.3 us -> 0 us
  between operations: 15.5 us -> 0.64 us
  blocking collectives: 14 us -> 0 us
  local copies, waits for them, and re-layouts: 7.03 us -> 0 us
    psum x3 -> x0, waiting for transfers between devices: 237 us -> none  [the longest x1 86.4 us: body(): back = lax.psum(transposed(blend, ortho), 'fsdp')]
    pallas_call x0 -> x2, Pallas kernels: none -> 71.5 us  [the longest x1 64.8 us: body(): pl.pallas_call(main_kernel, out_shape=(vmem((LOCAL_ROWS, LOCAL_COLS), F32...]
    dot_general x5 -> x0, matrix products: 60.6 us -> none  [the longest x2 20.7 us: transposed(): lax.dot_general(left, right, (((0,), (0,)), ((), ())), precision=HIGH, pr...]
    another operation x9 -> x0, other arithmetic: 53.7 us -> none  [the longest x6 33.9 us: body(): factor = jnp.linalg.cholesky(gram)]
    psum x1 -> x0, blocking collectives: 14 us -> none  [body(): squares = lax.psum(jnp.sum(back * back, axis=0), 'tp')]
    another operation x5 -> x0, matrix products: 5.67 us -> none  [the longest x3 3.52 us: body(): lax.linalg.triangular_solve(factor, projected, left_side=False, lower=Tru...]
    another operation x9 -> x0, local copies, waits for them, and re-layouts: 4.05 us -> none
  transfers between devices with their start and end apart: 3 -> 0, of which waited for: 3 -> 0; matrix products, arithmetic and copies ran while one was open for 0% -> 0% of each run, Pallas kernels for 0% -> 0%
where the time goes in v1:
time: 72.2 us; the launch traced here: 72.1 us
  Pallas kernels  71.5 us (99%)
    pallas_call x1, Pallas kernels, body(): pl.pallas_call(main_kernel, out_shape=(vmem((LOCAL_ROWS, LOCAL_COLS), F32...  64.8 us
    pallas_call x1, Pallas kernels, body(): pl.pallas_call(write_kernel, out_shape=(jax.ShapeDtypeStruct((LOCAL_ROWS,...  6.66 us

profile of v1, /device:TPU:1, one launch (start us, length us, event | category | flops | bytes accessed | tf_op | source)
XLA Modules:
  0.0 72.1 jit_solution(17112059605177853219)
XLA Ops:
  0.6 64.8 %transfers.1 = (f32[1792,1024]{1,0:T(8,128)S(1)}, f32[1792,256]{1,0:T(8,128)S(1)}, f32[256,1024]{1,0:T(8,128)S(1)}, f32[8,256]{1,0:T(8,128)S(1)}) custom-call(bf16[1792,1024]{1,0:T(8,128)(2,1)} %grad.1, f32[1792,1024]{1,0:T(8,128)} %mom.1, f32[1024,256]{1,0:T(8,128)} %basis.1), custom_call_target="tpu_custom_call" | custom-call | tf_op jit(solution)/shard_map/transfers/pallas_call | solution.py:664
  65.4 6.7 %outputs.1 = (f32[1792,1024]{1,0:T(8,128)}, f32[1024,256]{1,0:T(8,128)}, bf16[1792,1024]{1,0:T(8,128)(2,1)}) custom-call(f32[1792,1024]{1,0:T(8,128)S(1)} %get-tuple-element.7.blend, f32[1792,256]{1,0:T(8,128)S(1)} %get-tuple-element.8.ortho, f32[256,1024]{1,0:T(8,128)S(1)} %get-tuple-element.9.back, f32[8,256]{1,0:T(8,128)S(1)} %get-tuple-element.10.norm), custom_call_target="tpu_custom_call" | custom-call | tf_op jit(solution)/shard_map/outputs/pallas_call | solution.py:708

commit v2 on v1

--- a/solution.py
+++ b/solution.py
@@ -21,6 +21,7 @@
 HALF = 896
 PIECE = 224
 PART = 112
+STEP = 448
 WIDE = 512
 
 
@@ -117,19 +118,20 @@
     return jnp.concatenate(inverse, axis=0)
 
 
-def eliminate(k, m_ref):
+def eliminate(k, half, m_ref):
+    left = 128 * half
+    cols = slice(left, left + 384)
     rows = pl.ds(pl.multiple_of(32 * k, 32), 32)
-    tile = pl.ds(pl.multiple_of(128 * (k // 4), 128), 128)
-    d = pltpu.roll(m_ref[rows, tile], (128 - 32 * (k % 4)) % 128, 1)
+    d = pltpu.roll(m_ref[rows, left : left + 128], (128 - 32 * (k % 4)) % 128, 1)
     inverse = inverse_factor([d[8 * i : 8 * i + 8] for i in range(4)])
-    scaled = nn(inverse[:, :32], m_ref[rows, :], HIGH)
-    m_ref[rows, :] = scaled
+    scaled = nn(inverse[:, :32], m_ref[rows, cols], HIGH)
+    m_ref[rows, cols] = scaled
 
     @pl.when(k < 7)
     def _():
-        subl = lax.broadcasted_iota(jnp.int32, (RANK, 32), 0)
-        lower = jnp.where(subl >= 32 * k + 32, scaled[:, :RANK].T, 0.0)
-        m_ref[...] -= nn(lower, scaled, HIGH)
+        subl = lax.broadcasted_iota(jnp.int32, (RANK - left, 32), 0)
+        lower = jnp.where(subl >= 32 * k + 32 - left, scaled[:, : RANK - left].T, 0.0)
+        m_ref[left:, cols] -= nn(lower, scaled, HIGH)
 
 
 def main_kernel(
@@ -551,21 +553,27 @@
     gram_pair()
     w_steps_at = (w_step_2, None, w_step_3, w_step_4, None, w_step_5, w_step_6, w_step_7)
 
+    all_sent(N_HOP_A, 12, side_v.at[0])
+    all_sent(N_CORE, 8, part_v.at[0])
+    all_sent(GRAM_SUM, 33, sq_v.at[0])
+    all_sent(GRAM_CORE, 1, gram_part)
     arrive(gram_half(1 - c), GRAM_CORE)
     elim[:, :RANK] = gram[...]
     rr = lax.broadcasted_iota(jnp.int32, (RANK, RANK), 0)
     cc = lax.broadcasted_iota(jnp.int32, (RANK, RANK), 1)
     elim[:, RANK:] = jnp.where(rr == cc, 1.0, 0.0).astype(F32)
 
-    @pl.loop(0, 8)
-    def _(k):
-        eliminate(k, elim)
-        for at, step in enumerate(w_steps_at):
-            if step is not None:
-
-                @pl.when(k == at)
-                def _():
-                    both_halves(step)
+    for half in range(2):
+
+        @pl.loop(4 * half, 4 * half + 4)
+        def _(k):
+            eliminate(k, half, elim)
+            for at in range(4 * half, 4 * half + 4):
+                if w_steps_at[at] is not None:
+
+                    @pl.when(k == at)
+                    def _():
+                        both_halves(w_steps_at[at])
 
     f_hi, f_lo = split(elim[:, RANK:])
     factor = jnp.concatenate([f_hi, f_hi, f_lo], axis=1)
@@ -597,10 +605,6 @@
             jnp.concatenate([first, turned[:, 256:512], first], axis=0),
         )
 
-    all_sent(N_HOP_A, 12, side_v.at[0])
-    all_sent(N_CORE, 8, part_v.at[0])
-    all_sent(GRAM_SUM, 33, sq_v.at[0])
-    all_sent(GRAM_CORE, 1, gram_part)
     all_sent(W_HOP, 24, w_hop.at[0])
     all_sent(W_SUB, 12, w_sub.at[0])
 
@@ -623,8 +627,8 @@
     norms = norm[0:1, :]
 
     def copies(i):
-        rows = pl.ds(pl.multiple_of(i * PIECE, 32), PIECE)
-        rank_rows = pl.ds(pl.multiple_of(i * 128, 128), 128)
+        rows = pl.ds(pl.multiple_of(i * STEP, 64), STEP)
+        rank_rows = pl.ds(pl.multiple_of(i * 256, 256), 256)
         slot = i % 2
         return (
             pltpu.make_async_copy(mom_v.at[slot], mom_out.at[rows], sems.at[slot, 0]),
@@ -632,7 +636,7 @@
             pltpu.make_async_copy(basis_v.at[slot], basis_out.at[rank_rows], sems.at[slot, 2]),
         )
 
-    @pl.loop(0, 8)
+    @pl.loop(0, LOCAL_ROWS // STEP)
     def _(i):
         slot = i % 2
 
@@ -641,8 +645,8 @@
             for copy in copies(i - 2):
                 copy.wait()
 
-        rows = pl.ds(pl.multiple_of(i * PIECE, 32), PIECE)
-        cols = pl.ds(pl.multiple_of(i * 128, 128), 128)
+        rows = pl.ds(pl.multiple_of(i * STEP, 64), STEP)
+        cols = pl.ds(pl.multiple_of(i * 256, 256), 256)
         basis_v[slot] = back[:, cols].T * norms
         plain = ortho[rows, :]
         mom_v[slot] = blend[rows, :] - nn((0.05 * plain).astype(BF16), backs[:RANK])
@@ -651,7 +655,7 @@
         for copy in copies(i):
             copy.start()
 
-    for i in (6, 7):
+    for i in (2, 3):
         for copy in copies(i):
             copy.wait()
 
@@ -716,9 +720,9 @@
         out_specs=(anywhere,) * 3,
         scratch_shapes=[
             vmem((3 * RANK, LOCAL_COLS), BF16),
-            vmem((2, PIECE, LOCAL_COLS), F32),
-            vmem((2, 128, RANK), F32),
-            vmem((2, PIECE, LOCAL_COLS), BF16),
+            vmem((2, STEP, LOCAL_COLS), F32),
+            vmem((2, 256, RANK), F32),
+            vmem((2, STEP, LOCAL_COLS), BF16),
             pltpu.SemaphoreType.DMA((2, 3)),
         ],
         compiler_params=pltpu.CompilerParams(vmem_limit_bytes=32 * 2**20),

time: 72.2 us -> 71.4 us (0.989)
  Pallas kernels: 71.5 us -> 70.6 us
    pallas_call x1, Pallas kernels: 6.66 us -> 5.74 us  [body(): pl.pallas_call(write_kernel, out_shape=(jax.ShapeDtypeStruct((LOCAL_ROWS,...]
where the time goes in v2:
time: 71.4 us; the launch traced here: 71.3 us
  Pallas kernels  70.6 us (99%)
    pallas_call x1, Pallas kernels, body(): pl.pallas_call(main_kernel, out_shape=(vmem((LOCAL_ROWS, LOCAL_COLS), F32...  64.9 us
    pallas_call x1, Pallas kernels, body(): pl.pallas_call(write_kernel, out_shape=(jax.ShapeDtypeStruct((LOCAL_ROWS,...  5.74 us

profile of v2, /device:TPU:1, one launch (start us, length us, event | category | flops | bytes accessed | tf_op | source)
XLA Modules:
  0.0 71.3 jit_solution(12094742879340809682)
XLA Ops:
  0.6 64.9 %transfers.1 = (f32[1792,1024]{1,0:T(8,128)S(1)}, f32[1792,256]{1,0:T(8,128)S(1)}, f32[256,1024]{1,0:T(8,128)S(1)}, f32[8,256]{1,0:T(8,128)S(1)}) custom-call(bf16[1792,1024]{1,0:T(8,128)(2,1)} %grad.1, f32[1792,1024]{1,0:T(8,128)} %mom.1, f32[1024,256]{1,0:T(8,128)} %basis.1), custom_call_target="tpu_custom_call" | custom-call | tf_op jit(solution)/shard_map/transfers/pallas_call | solution.py:668
  65.5 5.7 %outputs.1 = (f32[1792,1024]{1,0:T(8,128)}, f32[1024,256]{1,0:T(8,128)}, bf16[1792,1024]{1,0:T(8,128)(2,1)}) custom-call(f32[1792,1024]{1,0:T(8,128)S(1)} %get-tuple-element.7.blend, f32[1792,256]{1,0:T(8,128)S(1)} %get-tuple-element.8.ortho, f32[256,1024]{1,0:T(8,128)S(1)} %get-tuple-element.9.back, f32[8,256]{1,0:T(8,128)S(1)} %get-tuple-element.10.norm), custom_call_target="tpu_custom_call" | custom-call | tf_op jit(solution)/shard_map/outputs/pallas_call | solution.py:712

commit v3 on v2

--- a/solution.py
+++ b/solution.py
@@ -163,6 +163,7 @@
     w_side,
     w_sub,
     w_full,
+    back_hi,
     sq_v,
     load_sem,
     send_sem,
@@ -301,15 +302,14 @@
         def _():
             add_core(2)
             send(part_v.at[5, b_rows], side_v.at[1], N_LEFT_B, right)
+            arrive(hop_v.at[0], N_HOP_A)
+            part_v[5, a_rows] += hop_v[0]
+            send(part_v.at[5, a_rows], side_v.at[0], N_LEFT_A, right)
+            arrive(hop_v.at[1], N_HOP_B)
+            part_v[3, b_rows] += hop_v[1]
+            send(part_v.at[3, b_rows], side_v.at[3], N_RIGHT_B, left)
 
     add_core(3)
-    arrive(hop_v.at[0], N_HOP_A)
-    part_v[5, a_rows] += hop_v[0]
-    send(part_v.at[5, a_rows], side_v.at[0], N_LEFT_A, right)
-    arrive(hop_v.at[1], N_HOP_B)
-    part_v[3, b_rows] += hop_v[1]
-    send(part_v.at[3, b_rows], side_v.at[3], N_RIGHT_B, left)
-
     my_row = piece_row(c, x)
     arrive(side_v.at[2], N_RIGHT_A)
     arrive(side_v.at[0], N_LEFT_A)
@@ -551,12 +551,9 @@
 
     both_halves(w_step_1)
     gram_pair()
-    w_steps_at = (w_step_2, None, w_step_3, w_step_4, None, w_step_5, w_step_6, w_step_7)
-
-    all_sent(N_HOP_A, 12, side_v.at[0])
-    all_sent(N_CORE, 8, part_v.at[0])
-    all_sent(GRAM_SUM, 33, sq_v.at[0])
-    all_sent(GRAM_CORE, 1, gram_part)
+    both_halves(w_step_2)
+    w_steps_at = (None, w_step_3, None, w_step_4, None, w_step_5, None, w_step_6)
+
     arrive(gram_half(1 - c), GRAM_CORE)
     elim[:, :RANK] = gram[...]
     rr = lax.broadcasted_iota(jnp.int32, (RANK, RANK), 0)
@@ -574,22 +571,6 @@
                     @pl.when(k == at)
                     def _():
                         both_halves(w_steps_at[at])
-
-    f_hi, f_lo = split(elim[:, RANK:])
-    factor = jnp.concatenate([f_hi, f_hi, f_lo], axis=1)
-    squares = jnp.zeros((RANK, 128), F32)
-    for n in range(4):
-        cols = slice(256 * n, 256 * n + 256)
-        w_hi, w_lo = split(w_full[:, cols])
-        back = nn(factor, jnp.concatenate([w_hi, w_lo, w_hi], axis=0))
-        back_out[:, cols] = back
-        squares = squares + (back[:, :128] * back[:, :128] + back[:, 128:] * back[:, 128:])
-    sq_v[t] = nt(jnp.ones((8, 128), F32), squares, HIGH)
-
-    @pl.loop(1, 8)
-    def _(d):
-        send(sq_v.at[t], sq_v.at[t], SQ + d - 1, {"fsdp": f, "tp": (t + d) % 8})
-
 
     t_hi, t_lo = split(elim[:, RANK:].T)
     turned[:, :256] = t_hi
@@ -605,6 +586,33 @@
             jnp.concatenate([first, turned[:, 256:512], first], axis=0),
         )
 
+    all_sent(N_HOP_A, 12, side_v.at[0])
+    all_sent(N_CORE, 8, part_v.at[0])
+    all_sent(GRAM_SUM, 33, sq_v.at[0])
+    all_sent(GRAM_CORE, 1, gram_part)
+    both_halves(w_step_7)
+    f_hi, f_lo = split(elim[:, RANK:])
+    factor = jnp.concatenate([f_hi, f_hi, f_lo], axis=1)
+    squares = jnp.zeros((RANK, 128), F32)
+    for n in range(4):
+        cols = slice(256 * n, 256 * n + 256)
+        w_hi, w_lo = split(w_full[:, cols])
+        back = nn(factor, jnp.concatenate([w_hi, w_lo, w_hi], axis=0))
+        back_out[:, cols] = back
+        back_hi[:, cols] = back.astype(BF16)
+        squares = squares + (back[:, :128] * back[:, :128] + back[:, 128:] * back[:, 128:])
+    sq_v[t] = nt(jnp.ones((8, 128), F32), squares, HIGH)
+
+    @pl.loop(1, 8)
+    def _(d):
+        send(sq_v.at[t], sq_v.at[t], SQ + d - 1, {"fsdp": f, "tp": (t + d) % 8})
+
+
+    @pl.loop(0, LOCAL_ROWS // STEP)
+    def _(i):
+        rows = pl.ds(pl.multiple_of(i * STEP, 64), STEP)
+        blend_out[rows, :] -= nn((0.05 * ortho_out[rows, :]).astype(BF16), back_hi[...])
+
     all_sent(W_HOP, 24, w_hop.at[0])
     all_sent(W_SUB, 12, w_sub.at[0])
 
@@ -617,8 +625,10 @@
 
 
 def write_kernel(
-    blend, ortho, back, norm, mom_out, basis_out, update_out, backs, mom_v, basis_v, update_v, sems
+    new_mom, ortho, back, norm, mom_out, basis_out, update_out, backs, basis_v, update_v, sems, mom_sem
 ):
+    mom_copy = pltpu.make_async_copy(new_mom, mom_out, mom_sem.at[0])
+    mom_copy.start()
     hi, lo = split(back[...])
     backs[:RANK] = hi
     backs[RANK : 2 * RANK] = lo
@@ -631,9 +641,8 @@
         rank_rows = pl.ds(pl.multiple_of(i * 256, 256), 256)
         slot = i % 2
         return (
-            pltpu.make_async_copy(mom_v.at[slot], mom_out.at[rows], sems.at[slot, 0]),
-            pltpu.make_async_copy(update_v.at[slot], update_out.at[rows], sems.at[slot, 1]),
-            pltpu.make_async_copy(basis_v.at[slot], basis_out.at[rank_rows], sems.at[slot, 2]),
+            pltpu.make_async_copy(update_v.at[slot], update_out.at[rows], sems.at[slot, 0]),
+            pltpu.make_async_copy(basis_v.at[slot], basis_out.at[rank_rows], sems.at[slot, 1]),
         )
 
     @pl.loop(0, LOCAL_ROWS // STEP)
@@ -648,9 +657,7 @@
         rows = pl.ds(pl.multiple_of(i * STEP, 64), STEP)
         cols = pl.ds(pl.multiple_of(i * 256, 256), 256)
         basis_v[slot] = back[:, cols].T * norms
-        plain = ortho[rows, :]
-        mom_v[slot] = blend[rows, :] - nn((0.05 * plain).astype(BF16), backs[:RANK])
-        hi, lo = split(plain * (scale * norms))
+        hi, lo = split(ortho[rows, :] * (scale * norms))
         update_v[slot] = nn(jnp.concatenate([hi, hi, lo], axis=1), backs[...]).astype(BF16)
         for copy in copies(i):
             copy.start()
@@ -658,6 +665,7 @@
     for i in (2, 3):
         for copy in copies(i):
             copy.wait()
+    mom_copy.wait()
 
 
 def body(gradient, momentum, basis):
@@ -697,6 +705,7 @@
             vmem((8, 32, WIDE), F32),
             vmem((6, 8, LOCAL_COLS), F32),
             vmem((RANK, LOCAL_COLS), F32),
+            vmem((RANK, LOCAL_COLS), BF16),
             vmem((8, 8, RANK), F32),
             pltpu.SemaphoreType.DMA((17,)),
             pltpu.SemaphoreType.DMA((NAMES.count,)),
@@ -720,10 +729,10 @@
         out_specs=(anywhere,) * 3,
         scratch_shapes=[
             vmem((3 * RANK, LOCAL_COLS), BF16),
-            vmem((2, STEP, LOCAL_COLS), F32),
             vmem((2, 256, RANK), F32),
             vmem((2, STEP, LOCAL_COLS), BF16),
-            pltpu.SemaphoreType.DMA((2, 3)),
+            pltpu.SemaphoreType.DMA((2, 2)),
+            pltpu.SemaphoreType.DMA((1,)),
         ],
         compiler_params=pltpu.CompilerParams(vmem_limit_bytes=32 * 2**20),
         name="outputs",

time: 71.4 us -> 71.6 us (level)
  no operation moved by 1% of the time
where the time goes in v3:
time: 71.6 us; the launch traced here: 71.4 us
  Pallas kernels  70.8 us (99%)
    pallas_call x1, Pallas kernels, body(): pl.pallas_call(main_kernel, out_shape=(vmem((LOCAL_ROWS, LOCAL_COLS), F32...  64.6 us
    pallas_call x1, Pallas kernels, body(): pl.pallas_call(write_kernel, out_shape=(jax.ShapeDtypeStruct((LOCAL_ROWS,...  6.23 us

profile of v3, /device:TPU:1, one launch (start us, length us, event | category | flops | bytes accessed | tf_op | source)
XLA Modules:
  0.0 71.4 jit_solution(17252306114426804417)
XLA Ops:
  0.6 64.6 %transfers.1 = (f32[1792,1024]{1,0:T(8,128)S(1)}, f32[1792,256]{1,0:T(8,128)S(1)}, f32[256,1024]{1,0:T(8,128)S(1)}, f32[8,256]{1,0:T(8,128)S(1)}) custom-call(bf16[1792,1024]{1,0:T(8,128)(2,1)} %grad.1, f32[1792,1024]{1,0:T(8,128)} %mom.1, f32[1024,256]{1,0:T(8,128)} %basis.1), custom_call_target="tpu_custom_call" | custom-call | tf_op jit(solution)/shard_map/transfers/pallas_call | solution.py:676
  65.2 6.2 %outputs.1 = (f32[1792,1024]{1,0:T(8,128)}, f32[1024,256]{1,0:T(8,128)}, bf16[1792,1024]{1,0:T(8,128)(2,1)}) custom-call(f32[1792,1024]{1,0:T(8,128)S(1)} %get-tuple-element.7.new_mom, f32[1792,256]{1,0:T(8,128)S(1)} %get-tuple-element.8.ortho, f32[256,1024]{1,0:T(8,128)S(1)} %get-tuple-element.9.back, f32[8,256]{1,0:T(8,128)S(1)} %get-tuple-element.10.norm), custom_call_target="tpu_custom_call" | custom-call | tf_op jit(solution)/shard_map/outputs/pallas_call | solution.py:721

commit v4 on v3

--- a/solution.py
+++ b/solution.py
@@ -49,12 +49,12 @@
 GRAM_ALL = NAMES.take(15)
 SQ = NAMES.take(7)
 GRAM_CORE = NAMES.take()
-W_HOP = NAMES.take(4)
-W_NEXT = NAMES.take(8)
-W_RING = NAMES.take(8)
-W_FAR = NAMES.take(4)
-W_SUB = NAMES.take(6)
-W_ALL = NAMES.take(6)
+W_HOP = NAMES.take(8)
+W_NEXT = NAMES.take(16)
+W_RING = NAMES.take(16)
+W_FAR = NAMES.take(8)
+W_SUB = NAMES.take(12)
+W_ALL = NAMES.take(12)
 
 
 def nn(a, b, precision=None):
@@ -447,18 +447,23 @@
             hi = hi_v[more, cols]
             w[:, cols] += nn(turned[...], jnp.concatenate([hi, lo_v[more, cols], hi], axis=0))
 
-    def places(h):
-        k, q = y + h * (z - y), z + h * (y - z)
+    def places(u):
+        k, q = y + u * (z - y), z + u * (y - z)
 
         def first(kk):
-            return f_dev(z * 4 + kk + h * (kk * 4 + y - z * 4 - kk))
+            return f_dev(z * 4 + kk + u * (kk * 4 + y - z * 4 - kk))
 
         def second(qq):
-            return f_dev(qq * 4 + y + h * (z * 4 + qq - qq * 4 - y))
+            return f_dev(qq * 4 + y + u * (z * 4 + qq - qq * 4 - y))
 
         return k, q, first, second
 
-    ca, cb = pl.ds(0, WIDE), pl.ds(WIDE, WIDE)
+    def cols_ab(u):
+        start = pl.multiple_of(WIDE * u, WIDE)
+        return pl.ds(start, 256), pl.ds(pl.multiple_of(start + 256, 256), 256)
+
+    def cols_u(u):
+        return pl.ds(pl.multiple_of(WIDE * u, WIDE), WIDE)
 
     def rows32(h, k):
         return pl.ds(pl.multiple_of(128 * h + 32 * k, 32), 32)
@@ -466,92 +471,105 @@
     def rows8(h, k, q):
         return pl.ds(pl.multiple_of(128 * h + 32 * k + 8 * q, 8), 8)
 
-    def w_step_1(h):
-        k, q, first, _ = places(h)
+    def w_step_1(h, u):
+        k, q, first, _ = places(u)
+        ca, cb = cols_ab(u)
+        i = 2 * h + u
         kr, kl, ko = (k + 1) % 4, (k + 3) % 4, (k + 2) % 4
-        send(w.at[rows32(h, ko), ca], w_hop.at[2 * h], W_HOP + 2 * h, first(kr))
-        send(w.at[rows32(h, ko), cb], w_hop.at[2 * h + 1], W_HOP + 2 * h + 1, first(kl))
-        send(w.at[rows32(h, kr), cb], w_side.at[4 * h + 1], W_NEXT + 4 * h + 1, first(kr))
-        send(w.at[rows32(h, kl), ca], w_side.at[4 * h + 2], W_NEXT + 4 * h + 2, first(kl))
-
-    def w_step_2(h):
-        k, q, first, _ = places(h)
+        send(w.at[rows32(h, ko), ca], w_hop.at[2 * i], W_HOP + 2 * i, first(kr))
+        send(w.at[rows32(h, ko), cb], w_hop.at[2 * i + 1], W_HOP + 2 * i + 1, first(kl))
+        send(w.at[rows32(h, kr), cb], w_side.at[4 * i + 1], W_NEXT + 4 * i + 1, first(kr))
+        send(w.at[rows32(h, kl), ca], w_side.at[4 * i + 2], W_NEXT + 4 * i + 2, first(kl))
+
+    def w_step_2(h, u):
+        k, q, first, _ = places(u)
+        ca, cb = cols_ab(u)
+        i = 2 * h + u
         kr, kl = (k + 1) % 4, (k + 3) % 4
-        arrive(w_hop.at[2 * h], W_HOP + 2 * h)
-        w[rows32(h, kr), ca] += w_hop[2 * h]
-        send(w.at[rows32(h, kr), ca], w_side.at[4 * h], W_NEXT + 4 * h, first(kr))
-        arrive(w_hop.at[2 * h + 1], W_HOP + 2 * h + 1)
-        w[rows32(h, kl), cb] += w_hop[2 * h + 1]
-        send(w.at[rows32(h, kl), cb], w_side.at[4 * h + 3], W_NEXT + 4 * h + 3, first(kl))
-
-    def w_step_3(h):
-        k, q, _, second = places(h)
+        arrive(w_hop.at[2 * i], W_HOP + 2 * i)
+        w[rows32(h, kr), ca] += w_hop[2 * i]
+        send(w.at[rows32(h, kr), ca], w_side.at[4 * i], W_NEXT + 4 * i, first(kr))
+        arrive(w_hop.at[2 * i + 1], W_HOP + 2 * i + 1)
+        w[rows32(h, kl), cb] += w_hop[2 * i + 1]
+        send(w.at[rows32(h, kl), cb], w_side.at[4 * i + 3], W_NEXT + 4 * i + 3, first(kl))
+
+    def w_step_3(h, u):
+        k, q, _, second = places(u)
+        ca, cb = cols_ab(u)
+        i = 2 * h + u
         for s in range(4):
-            arrive(w_side.at[4 * h + s], W_NEXT + 4 * h + s)
-        w[rows32(h, k), ca] += w_side[4 * h] + w_side[4 * h + 2]
-        w[rows32(h, k), cb] += w_side[4 * h + 1] + w_side[4 * h + 3]
+            arrive(w_side.at[4 * i + s], W_NEXT + 4 * i + s)
+        w[rows32(h, k), ca] += w_side[4 * i] + w_side[4 * i + 2]
+        w[rows32(h, k), cb] += w_side[4 * i + 1] + w_side[4 * i + 3]
 
         @pl.loop(1, 4)
         def _(d):
-            to, slot = (q + d) % 4, 3 * h + d - 1
-            send(w.at[rows8(h, k, to)], w_sub.at[slot], W_SUB + slot, second(to))
-
-    def w_step_4(h):
-        k, q, _, second = places(h)
+            to, slot = (q + d) % 4, 3 * i + d - 1
+            send(w.at[rows8(h, k, to), cols_u(u)], w_sub.at[slot], W_SUB + slot, second(to))
+
+    def w_step_4(h, u):
+        k, q, _, second = places(u)
+        i = 2 * h + u
 
         @pl.loop(0, 3)
         def _(d):
-            arrive(w_sub.at[3 * h + d], W_SUB + 3 * h + d)
-
-        w_full[rows8(h, k, q), :] = (w[rows8(h, k, q), :] + w_sub[3 * h]) + (
-            w_sub[3 * h + 1] + w_sub[3 * h + 2]
+            arrive(w_sub.at[3 * i + d], W_SUB + 3 * i + d)
+
+        w_full[rows8(h, k, q), cols_u(u)] = (w[rows8(h, k, q), cols_u(u)] + w_sub[3 * i]) + (
+            w_sub[3 * i + 1] + w_sub[3 * i + 2]
         )
 
         @pl.loop(1, 4)
         def _(d):
-            mine = w_full.at[rows8(h, k, q)]
-            send(mine, mine, W_ALL + 3 * h + d - 1, second((q + d) % 4))
-
-    def w_step_5(h):
-        k, q, first, _ = places(h)
+            mine = w_full.at[rows8(h, k, q), cols_u(u)]
+            send(mine, mine, W_ALL + 3 * i + d - 1, second((q + d) % 4))
+
+    def w_step_5(h, u):
+        k, q, first, _ = places(u)
+        ca, cb = cols_ab(u)
+        i = 2 * h + u
         dr, dl = first((k + 1) % 4), first((k + 3) % 4)
 
         @pl.loop(1, 4)
         def _(d):
-            arrive(w_full.at[rows8(h, k, (q + 4 - d) % 4)], W_ALL + 3 * h + d - 1)
+            arrive(w_full.at[rows8(h, k, (q + 4 - d) % 4), cols_u(u)], W_ALL + 3 * i + d - 1)
 
         mine_a, mine_b = w_full.at[rows32(h, k), ca], w_full.at[rows32(h, k), cb]
-        send(mine_a, mine_a, W_RING + 4 * h, dr)
-        send(mine_b, mine_b, W_RING + 4 * h + 3, dl)
-        send(mine_b, mine_b, W_RING + 4 * h + 1, dr)
-        send(mine_a, mine_a, W_RING + 4 * h + 2, dl)
-
-    def w_step_6(h):
-        k, q, first, _ = places(h)
+        send(mine_a, mine_a, W_RING + 4 * i, dr)
+        send(mine_b, mine_b, W_RING + 4 * i + 3, dl)
+        send(mine_b, mine_b, W_RING + 4 * i + 1, dr)
+        send(mine_a, mine_a, W_RING + 4 * i + 2, dl)
+
+    def w_step_6(h, u):
+        k, q, first, _ = places(u)
+        ca, cb = cols_ab(u)
+        i = 2 * h + u
         kr, kl = (k + 1) % 4, (k + 3) % 4
         from_left = w_full.at[rows32(h, kl), ca]
-        arrive(from_left, W_RING + 4 * h)
-        send(from_left, from_left, W_FAR + 2 * h, first(kr))
+        arrive(from_left, W_RING + 4 * i)
+        send(from_left, from_left, W_FAR + 2 * i, first(kr))
         from_right = w_full.at[rows32(h, kr), cb]
-        arrive(from_right, W_RING + 4 * h + 3)
-        send(from_right, from_right, W_FAR + 2 * h + 1, first(kl))
-
-    def w_step_7(h):
-        k = places(h)[0]
+        arrive(from_right, W_RING + 4 * i + 3)
+        send(from_right, from_right, W_FAR + 2 * i + 1, first(kl))
+
+    def w_step_7(h, u):
+        k = places(u)[0]
+        ca, cb = cols_ab(u)
+        i = 2 * h + u
         kr, kl, ko = (k + 1) % 4, (k + 3) % 4, (k + 2) % 4
-        arrive(w_full.at[rows32(h, kl), cb], W_RING + 4 * h + 1)
-        arrive(w_full.at[rows32(h, kr), ca], W_RING + 4 * h + 2)
-        arrive(w_full.at[rows32(h, ko), ca], W_FAR + 2 * h)
-        arrive(w_full.at[rows32(h, ko), cb], W_FAR + 2 * h + 1)
-
-    def both_halves(step):
-        @pl.loop(0, 2)
-        def _(h):
-            step(h)
-
-    both_halves(w_step_1)
+        arrive(w_full.at[rows32(h, kl), cb], W_RING + 4 * i + 1)
+        arrive(w_full.at[rows32(h, kr), ca], W_RING + 4 * i + 2)
+        arrive(w_full.at[rows32(h, ko), ca], W_FAR + 2 * i)
+        arrive(w_full.at[rows32(h, ko), cb], W_FAR + 2 * i + 1)
+
+    def all_parts(step):
+        @pl.loop(0, 4)
+        def _(i):
+            step(i // 2, i % 2)
+
+    all_parts(w_step_1)
     gram_pair()
-    both_halves(w_step_2)
+    all_parts(w_step_2)
     w_steps_at = (None, w_step_3, None, w_step_4, None, w_step_5, None, w_step_6)
 
     arrive(gram_half(1 - c), GRAM_CORE)
@@ -570,7 +588,7 @@
 
                     @pl.when(k == at)
                     def _():
-                        both_halves(w_steps_at[at])
+                        all_parts(w_steps_at[at])
 
     t_hi, t_lo = split(elim[:, RANK:].T)
     turned[:, :256] = t_hi
@@ -590,7 +608,7 @@
     all_sent(N_CORE, 8, part_v.at[0])
     all_sent(GRAM_SUM, 33, sq_v.at[0])
     all_sent(GRAM_CORE, 1, gram_part)
-    both_halves(w_step_7)
+    all_parts(w_step_7)
     f_hi, f_lo = split(elim[:, RANK:])
     factor = jnp.concatenate([f_hi, f_hi, f_lo], axis=1)
     squares = jnp.zeros((RANK, 128), F32)
@@ -613,8 +631,8 @@
         rows = pl.ds(pl.multiple_of(i * STEP, 64), STEP)
         blend_out[rows, :] -= nn((0.05 * ortho_out[rows, :]).astype(BF16), back_hi[...])
 
-    all_sent(W_HOP, 24, w_hop.at[0])
-    all_sent(W_SUB, 12, w_sub.at[0])
+    all_sent(W_HOP, 48, w_hop.at[0])
+    all_sent(W_SUB, 24, w_sub.at[0])
 
     @pl.loop(1, 8)
     def _(d):
@@ -627,8 +645,12 @@
 def write_kernel(
     new_mom, ortho, back, norm, mom_out, basis_out, update_out, backs, basis_v, update_v, sems, mom_sem
 ):
-    mom_copy = pltpu.make_async_copy(new_mom, mom_out, mom_sem.at[0])
-    mom_copy.start()
+    def mom_copy(i):
+        rows = pl.ds(PIECE * i, PIECE)
+        return pltpu.make_async_copy(new_mom.at[rows], mom_out.at[rows], mom_sem.at[i])
+
+    for i in range(8):
+        mom_copy(i).start(priority=i % 2)
     hi, lo = split(back[...])
     backs[:RANK] = hi
     backs[RANK : 2 * RANK] = lo
@@ -665,7 +687,8 @@
     for i in (2, 3):
         for copy in copies(i):
             copy.wait()
-    mom_copy.wait()
+    for i in range(8):
+        mom_copy(i).wait()
 
 
 def body(gradient, momentum, basis):
@@ -701,9 +724,9 @@
             vmem((RANK, 2 * RANK), F32),
             vmem((RANK, 3 * 256), BF16),
             vmem((RANK, LOCAL_COLS), F32),
-            vmem((4, 32, WIDE), F32),
-            vmem((8, 32, WIDE), F32),
-            vmem((6, 8, LOCAL_COLS), F32),
+            vmem((8, 32, 256), F32),
+            vmem((16, 32, 256), F32),
+            vmem((12, 8, WIDE), F32),
             vmem((RANK, LOCAL_COLS), F32),
             vmem((RANK, LOCAL_COLS), BF16),
             vmem((8, 8, RANK), F32),
@@ -732,7 +755,7 @@
             vmem((2, 256, RANK), F32),
             vmem((2, STEP, LOCAL_COLS), BF16),
             pltpu.SemaphoreType.DMA((2, 2)),
-            pltpu.SemaphoreType.DMA((1,)),
+            pltpu.SemaphoreType.DMA((8,)),
         ],
         compiler_params=pltpu.CompilerParams(vmem_limit_bytes=32 * 2**20),
         name="outputs",

time: 71.6 us -> 70.9 us (level)
  no operation moved by 1% of the time
where the time goes in v4:
time: 70.9 us; the launch traced here: 70.8 us
  Pallas kernels  70.1 us (99%)
    pallas_call x1, Pallas kernels, body(): pl.pallas_call(main_kernel, out_shape=(vmem((LOCAL_ROWS, LOCAL_COLS), F32...  64.6 us
    pallas_call x1, Pallas kernels, body(): pl.pallas_call(write_kernel, out_shape=(jax.ShapeDtypeStruct((LOCAL_ROWS,...  5.53 us

profile of v4, /device:TPU:1, one launch (start us, length us, event | category | flops | bytes accessed | tf_op | source)
XLA Modules:
  0.0 70.8 jit_solution(1230050100363057388)
XLA Ops:
  0.6 64.6 %transfers.1 = (f32[1792,1024]{1,0:T(8,128)S(1)}, f32[1792,256]{1,0:T(8,128)S(1)}, f32[256,1024]{1,0:T(8,128)S(1)}, f32[8,256]{1,0:T(8,128)S(1)}) custom-call(bf16[1792,1024]{1,0:T(8,128)(2,1)} %grad.1, f32[1792,1024]{1,0:T(8,128)} %mom.1, f32[1024,256]{1,0:T(8,128)} %basis.1), custom_call_target="tpu_custom_call" | custom-call | tf_op jit(solution)/shard_map/transfers/pallas_call | solution.py:699
  65.2 5.5 %outputs.1 = (f32[1792,1024]{1,0:T(8,128)}, f32[1024,256]{1,0:T(8,128)}, bf16[1792,1024]{1,0:T(8,128)(2,1)}) custom-call(f32[1792,1024]{1,0:T(8,128)S(1)} %get-tuple-element.7.new_mom, f32[1792,256]{1,0:T(8,128)S(1)} %get-tuple-element.8.ortho, f32[256,1024]{1,0:T(8,128)S(1)} %get-tuple-element.9.back, f32[8,256]{1,0:T(8,128)S(1)} %get-tuple-element.10.norm), custom_call_target="tpu_custom_call" | custom-call | tf_op jit(solution)/shard_map/outputs/pallas_call | solution.py:744

commit v5 on v4

--- a/solution.py
+++ b/solution.py
@@ -163,7 +163,6 @@
     w_side,
     w_sub,
     w_full,
-    back_hi,
     sq_v,
     load_sem,
     send_sem,
@@ -570,7 +569,7 @@
     all_parts(w_step_1)
     gram_pair()
     all_parts(w_step_2)
-    w_steps_at = (None, w_step_3, None, w_step_4, None, w_step_5, None, w_step_6)
+    w_steps_at = (w_step_3, None, w_step_4, None, w_step_5, None, w_step_6, w_step_7)
 
     arrive(gram_half(1 - c), GRAM_CORE)
     elim[:, :RANK] = gram[...]
@@ -589,6 +588,22 @@
                     @pl.when(k == at)
                     def _():
                         all_parts(w_steps_at[at])
+
+    f_hi, f_lo = split(elim[:, RANK:])
+    factor = jnp.concatenate([f_hi, f_hi, f_lo], axis=1)
+    squares = jnp.zeros((RANK, 128), F32)
+    for n in range(4):
+        cols = slice(256 * n, 256 * n + 256)
+        w_hi, w_lo = split(w_full[:, cols])
+        back = nn(factor, jnp.concatenate([w_hi, w_lo, w_hi], axis=0))
+        back_out[:, cols] = back
+        squares = squares + (back[:, :128] * back[:, :128] + back[:, 128:] * back[:, 128:])
+    sq_v[t] = nt(jnp.ones((8, 128), F32), squares, HIGH)
+
+    @pl.loop(1, 8)
+    def _(d):
+        send(sq_v.at[t], sq_v.at[t], SQ + d - 1, {"fsdp": f, "tp": (t + d) % 8})
+
 
     t_hi, t_lo = split(elim[:, RANK:].T)
     turned[:, :256] = t_hi
@@ -608,29 +623,6 @@
     all_sent(N_CORE, 8, part_v.at[0])
     all_sent(GRAM_SUM, 33, sq_v.at[0])
     all_sent(GRAM_CORE, 1, gram_part)
-    all_parts(w_step_7)
-    f_hi, f_lo = split(elim[:, RANK:])
-    factor = jnp.concatenate([f_hi, f_hi, f_lo], axis=1)
-    squares = jnp.zeros((RANK, 128), F32)
-    for n in range(4):
-        cols = slice(256 * n, 256 * n + 256)
-        w_hi, w_lo = split(w_full[:, cols])
-        back = nn(factor, jnp.concatenate([w_hi, w_lo, w_hi], axis=0))
-        back_out[:, cols] = back
-        back_hi[:, cols] = back.astype(BF16)
-        squares = squares + (back[:, :128] * back[:, :128] + back[:, 128:] * back[:, 128:])
-    sq_v[t] = nt(jnp.ones((8, 128), F32), squares, HIGH)
-
-    @pl.loop(1, 8)
-    def _(d):
-        send(sq_v.at[t], sq_v.at[t], SQ + d - 1, {"fsdp": f, "tp": (t + d) % 8})
-
-
-    @pl.loop(0, LOCAL_ROWS // STEP)
-    def _(i):
-        rows = pl.ds(pl.multiple_of(i * STEP, 64), STEP)
-        blend_out[rows, :] -= nn((0.05 * ortho_out[rows, :]).astype(BF16), back_hi[...])
-
     all_sent(W_HOP, 48, w_hop.at[0])
     all_sent(W_SUB, 24, w_sub.at[0])
 
@@ -643,14 +635,8 @@
 
 
 def write_kernel(
-    new_mom, ortho, back, norm, mom_out, basis_out, update_out, backs, basis_v, update_v, sems, mom_sem
+    blend, ortho, back, norm, mom_out, basis_out, update_out, backs, mom_v, basis_v, update_v, sems
 ):
-    def mom_copy(i):
-        rows = pl.ds(PIECE * i, PIECE)
-        return pltpu.make_async_copy(new_mom.at[rows], mom_out.at[rows], mom_sem.at[i])
-
-    for i in range(8):
-        mom_copy(i).start(priority=i % 2)
     hi, lo = split(back[...])
     backs[:RANK] = hi
     backs[RANK : 2 * RANK] = lo
@@ -659,13 +645,18 @@
     norms = norm[0:1, :]
 
     def copies(i):
-        rows = pl.ds(pl.multiple_of(i * STEP, 64), STEP)
+        slot = i % 2
+        found = []
+        for p in range(2):
+            rows = pl.ds(pl.multiple_of(i * STEP + p * PIECE, 32), PIECE)
+            here = pl.ds(p * PIECE, PIECE)
+            found.append(pltpu.make_async_copy(mom_v.at[slot, here], mom_out.at[rows], sems.at[slot, p]))
+            found.append(
+                pltpu.make_async_copy(update_v.at[slot, here], update_out.at[rows], sems.at[slot, 2 + p])
+            )
         rank_rows = pl.ds(pl.multiple_of(i * 256, 256), 256)
-        slot = i % 2
-        return (
-            pltpu.make_async_copy(update_v.at[slot], update_out.at[rows], sems.at[slot, 0]),
-            pltpu.make_async_copy(basis_v.at[slot], basis_out.at[rank_rows], sems.at[slot, 1]),
-        )
+        found.append(pltpu.make_async_copy(basis_v.at[slot], basis_out.at[rank_rows], sems.at[slot, 4]))
+        return found
 
     @pl.loop(0, LOCAL_ROWS // STEP)
     def _(i):
@@ -679,16 +670,20 @@
         rows = pl.ds(pl.multiple_of(i * STEP, 64), STEP)
         cols = pl.ds(pl.multiple_of(i * 256, 256), 256)
         basis_v[slot] = back[:, cols].T * norms
-        hi, lo = split(ortho[rows, :] * (scale * norms))
+        plain = ortho[rows, :]
+        mom_v[slot] = blend[rows, :] - nn((0.05 * plain).astype(BF16), backs[:RANK])
+        mom_a, update_a, mom_b, update_b, basis_copy = copies(i)
+        mom_a.start()
+        mom_b.start(priority=1)
+        basis_copy.start()
+        hi, lo = split(plain * (scale * norms))
         update_v[slot] = nn(jnp.concatenate([hi, hi, lo], axis=1), backs[...]).astype(BF16)
-        for copy in copies(i):
-            copy.start()
+        update_a.start()
+        update_b.start(priority=1)
 
     for i in (2, 3):
         for copy in copies(i):
             copy.wait()
-    for i in range(8):
-        mom_copy(i).wait()
 
 
 def body(gradient, momentum, basis):
@@ -728,7 +723,6 @@
             vmem((16, 32, 256), F32),
             vmem((12, 8, WIDE), F32),
             vmem((RANK, LOCAL_COLS), F32),
-            vmem((RANK, LOCAL_COLS), BF16),
             vmem((8, 8, RANK), F32),
             pltpu.SemaphoreType.DMA((17,)),
             pltpu.SemaphoreType.DMA((NAMES.count,)),
@@ -752,10 +746,10 @@
         out_specs=(anywhere,) * 3,
         scratch_shapes=[
             vmem((3 * RANK, LOCAL_COLS), BF16),
+            vmem((2, STEP, LOCAL_COLS), F32),
             vmem((2, 256, RANK), F32),
             vmem((2, STEP, LOCAL_COLS), BF16),
-            pltpu.SemaphoreType.DMA((2, 2)),
-            pltpu.SemaphoreType.DMA((8,)),
+            pltpu.SemaphoreType.DMA((2, 5)),
         ],
         compiler_params=pltpu.CompilerParams(vmem_limit_bytes=32 * 2**20),
         name="outputs",

time: 70.9 us -> 70.7 us (level)
  no operation moved by 1% of the time
where the time goes in v5:
time: 70.7 us; the launch traced here: 70.6 us
  Pallas kernels  69.9 us (99%)
    pallas_call x1, Pallas kernels, body(): pl.pallas_call(main_kernel, out_shape=(vmem((LOCAL_ROWS, LOCAL_COLS), F32...  64.2 us
    pallas_call x1, Pallas kernels, body(): pl.pallas_call(write_kernel, out_shape=(jax.ShapeDtypeStruct((LOCAL_ROWS,...  5.73 us

profile of v5, /device:TPU:1, one launch (start us, length us, event | category | flops | bytes accessed | tf_op | source)
XLA Modules:
  0.0 70.6 jit_solution(13730341136055940513)
XLA Ops:
  0.6 64.2 %transfers.1 = (f32[1792,1024]{1,0:T(8,128)S(1)}, f32[1792,256]{1,0:T(8,128)S(1)}, f32[256,1024]{1,0:T(8,128)S(1)}, f32[8,256]{1,0:T(8,128)S(1)}) custom-call(bf16[1792,1024]{1,0:T(8,128)(2,1)} %grad.1, f32[1792,1024]{1,0:T(8,128)} %mom.1, f32[1024,256]{1,0:T(8,128)} %basis.1), custom_call_target="tpu_custom_call" | custom-call | tf_op jit(solution)/shard_map/transfers/pallas_call | solution.py:694
  64.8 5.7 %outputs.1 = (f32[1792,1024]{1,0:T(8,128)}, f32[1024,256]{1,0:T(8,128)}, bf16[1792,1024]{1,0:T(8,128)(2,1)}) custom-call(f32[1792,1024]{1,0:T(8,128)S(1)} %get-tuple-element.7.blend, f32[1792,256]{1,0:T(8,128)S(1)} %get-tuple-element.8.ortho, f32[256,1024]{1,0:T(8,128)S(1)} %get-tuple-element.9.back, f32[8,256]{1,0:T(8,128)S(1)} %get-tuple-element.10.norm), custom_call_target="tpu_custom_call" | custom-call | tf_op jit(solution)/shard_map/outputs/pallas_call | solution.py:738

commit v6 on v5

--- a/solution.py
+++ b/solution.py
@@ -402,15 +402,14 @@
         @pl.when(g == 1)
         def _():
             arrive(whole_of(1 - c, x), G_CORE)
-            gram_start()
-
-        @pl.when(g == 2)
-        def _():
             arrive(part_of(c, xl, 0), G_LEFT_A)
             send_part(xl, 0, G_OPP_A, right)
             arrive(part_of(c, xr, 1), G_RIGHT_B)
             send_part(xr, 1, G_OPP_B, left)
-            gram_across()
+            gram_start()
+
+        @pl.when(g == 2)
+        def _():
             arrive(part_of(c, xr, 0), G_RIGHT_A)
             send_whole(xr, G_CORE + 1)
             arrive(part_of(c, xl, 1), G_LEFT_B)
@@ -421,10 +420,10 @@
             arrive(part_of(c, xo, 0), G_OPP_A)
             arrive(part_of(c, xo, 1), G_OPP_B)
             send_whole(xo, G_CORE + 3)
-            gram_round()
 
         @pl.when(g == 5)
         def _():
+            gram_across()
             arrive(whole_of(1 - c, xr), G_CORE + 1)
 
         @pl.when(g == 6)
@@ -567,8 +566,9 @@
             step(i // 2, i % 2)
 
     all_parts(w_step_1)
+    gram_round()
+    all_parts(w_step_2)
     gram_pair()
-    all_parts(w_step_2)
     w_steps_at = (w_step_3, None, w_step_4, None, w_step_5, None, w_step_6, w_step_7)
 
     arrive(gram_half(1 - c), GRAM_CORE)

time: 70.7 us -> 72.1 us (1.020)
  Pallas kernels: 69.9 us -> 71.4 us
    pallas_call x1, Pallas kernels: 64.2 us -> 65.6 us  [body(): pl.pallas_call(main_kernel, out_shape=(vmem((LOCAL_ROWS, LOCAL_COLS), F32...]
where the time goes in v6:
time: 72.1 us; the launch traced here: 72 us
  Pallas kernels  71.4 us (99%)
    pallas_call x1, Pallas kernels, body(): pl.pallas_call(main_kernel, out_shape=(vmem((LOCAL_ROWS, LOCAL_COLS), F32...  65.6 us
    pallas_call x1, Pallas kernels, body(): pl.pallas_call(write_kernel, out_shape=(jax.ShapeDtypeStruct((LOCAL_ROWS,...  5.73 us

profile of v6, /device:TPU:1, one launch (start us, length us, event | category | flops | bytes accessed | tf_op | source)
XLA Modules:
  0.0 72.0 jit_solution(11601226031902652164)
XLA Ops:
  0.6 65.6 %transfers.1 = (f32[1792,1024]{1,0:T(8,128)S(1)}, f32[1792,256]{1,0:T(8,128)S(1)}, f32[256,1024]{1,0:T(8,128)S(1)}, f32[8,256]{1,0:T(8,128)S(1)}) custom-call(bf16[1792,1024]{1,0:T(8,128)(2,1)} %grad.1, f32[1792,1024]{1,0:T(8,128)} %mom.1, f32[1024,256]{1,0:T(8,128)} %basis.1), custom_call_target="tpu_custom_call" | custom-call | tf_op jit(solution)/shard_map/transfers/pallas_call | solution.py:694
  66.3 5.7 %outputs.1 = (f32[1792,1024]{1,0:T(8,128)}, f32[1024,256]{1,0:T(8,128)}, bf16[1792,1024]{1,0:T(8,128)(2,1)}) custom-call(f32[1792,1024]{1,0:T(8,128)S(1)} %get-tuple-element.7.blend, f32[1792,256]{1,0:T(8,128)S(1)} %get-tuple-element.8.ortho, f32[256,1024]{1,0:T(8,128)S(1)} %get-tuple-element.9.back, f32[8,256]{1,0:T(8,128)S(1)} %get-tuple-element.10.norm), custom_call_target="tpu_custom_call" | custom-call | tf_op jit(solution)/shard_map/outputs/pallas_call | solution.py:738

commit v7 on v5

--- a/solution.py
+++ b/solution.py
@@ -100,22 +100,44 @@
         for k in range(8 * n)
     ]
     inverse = [jnp.where(lane == sub + 8 * i, 1.0, 0.0) for i in range(n)]
-    for j in range(8 * n):
-        g, r = j // 8, j % 8
-        pivot = row_copy(col[j][g], r)
-        inv = 1.0 / pivot
-        row = row_copy(inverse[g], r)
-        entry = {k: row_copy(col[j][k // 8], k % 8) for k in range(j + 1, 8 * n)}
-        mult = [None if i < g else col[j][i] * inv for i in range(n)]
-        if r < 7:
-            mult[g] = jnp.where(sub > r, mult[g], 0.0)
-        for k in range(j + 1, 8 * n):
+    for g in range(n):
+        entry = [[row_copy(col[8 * g + j][g], i) for j in range(i + 1)] for i in range(8)]
+        rows = [row_copy(inverse[g], j) for j in range(8)]
+        inv, mult = [], [[None] * 8 for _ in range(8)]
+        for j in range(8):
+            inv.append(1.0 / entry[j][j])
+            for k in range(j + 1, 8):
+                mult[k][j] = entry[k][j] * inv[j]
+                for i in range(k, 8):
+                    entry[i][k] = entry[i][k] - entry[i][j] * mult[k][j]
+                rows[k] = rows[k] - mult[k][j] * rows[j]
+        final = jnp.zeros((8, 128), F32)
+        for j in range(8):
+            final = jnp.where(sub == j, rows[j] * lax.rsqrt(entry[j][j]), final)
+        inverse[g] = final
+        below = {}
+        for i in range(g + 1, n):
+            c = [col[8 * g + j][i] for j in range(8)]
+            for j in range(8):
+                for k in range(j + 1, 8):
+                    c[k] = c[k] - c[j] * mult[k][j]
+            below[i] = (c, [c[j] * inv[j] for j in range(8)])
+        for k in range(8 * g + 8, 8 * n):
+            across = [row_copy(below[k // 8][0][j], k % 8) for j in range(8)]
             for i in range(k // 8, n):
-                col[k][i] = col[k][i] - mult[i] * entry[k]
-        for i in range(g + (r == 7), n):
-            inverse[i] = inverse[i] - mult[i] * row
-        inverse[g] = jnp.where(sub == r, row * lax.rsqrt(pivot), inverse[g])
+                for j in range(8):
+                    col[k][i] = col[k][i] - below[i][1][j] * across[j]
+        for i in range(g + 1, n):
+            for j in range(8):
+                inverse[i] = inverse[i] - below[i][1][j] * rows[j]
     return jnp.concatenate(inverse, axis=0)
+
+
+def split3(x):
+    first = x.astype(BF16)
+    rest = x - first.astype(F32)
+    second = rest.astype(BF16)
+    return first, second, (rest - second.astype(F32)).astype(BF16)
 
 
 def eliminate(k, half, m_ref):
@@ -129,9 +151,13 @@
 
     @pl.when(k < 7)
     def _():
-        subl = lax.broadcasted_iota(jnp.int32, (RANK - left, 32), 0)
-        lower = jnp.where(subl >= 32 * k + 32 - left, scaled[:, : RANK - left].T, 0.0)
-        m_ref[left:, cols] -= nn(lower, scaled, HIGH)
+        lane = lax.broadcasted_iota(jnp.int32, (32, RANK - left), 1)
+        lower = jnp.where(lane >= 32 * k + 32 - left, scaled[:, : RANK - left], 0.0)
+        a, b, c = split3(lower)
+        d, e, f = split3(scaled)
+        m_ref[left:, cols] -= tn(
+            jnp.concatenate([a, a, b, a, b, c], axis=0), jnp.concatenate([d, e, d, f, e, d], axis=0)
+        )
 
 
 def main_kernel(

time: 70.7 us -> 70.5 us (level)
  no operation moved by 1% of the time
where the time goes in v7:
time: 70.5 us; the launch traced here: 70.4 us
  Pallas kernels  69.7 us (99%)
    pallas_call x1, Pallas kernels, body(): pl.pallas_call(main_kernel, out_shape=(vmem((LOCAL_ROWS, LOCAL_COLS), F32...  64 us
    pallas_call x1, Pallas kernels, body(): pl.pallas_call(write_kernel, out_shape=(jax.ShapeDtypeStruct((LOCAL_ROWS,...  5.73 us

profile of v7, /device:TPU:1, one launch (start us, length us, event | category | flops | bytes accessed | tf_op | source)
XLA Modules:
  0.0 70.4 jit_solution(3900956155021782260)
XLA Ops:
  0.6 64.0 %transfers.1 = (f32[1792,1024]{1,0:T(8,128)S(1)}, f32[1792,256]{1,0:T(8,128)S(1)}, f32[256,1024]{1,0:T(8,128)S(1)}, f32[8,256]{1,0:T(8,128)S(1)}) custom-call(bf16[1792,1024]{1,0:T(8,128)(2,1)} %grad.1, f32[1792,1024]{1,0:T(8,128)} %mom.1, f32[1024,256]{1,0:T(8,128)} %basis.1), custom_call_target="tpu_custom_call" | custom-call | tf_op jit(solution)/shard_map/transfers/pallas_call | solution.py:720
  64.6 5.7 %outputs.1 = (f32[1792,1024]{1,0:T(8,128)}, f32[1024,256]{1,0:T(8,128)}, bf16[1792,1024]{1,0:T(8,128)(2,1)}) custom-call(f32[1792,1024]{1,0:T(8,128)S(1)} %get-tuple-element.7.blend, f32[1792,256]{1,0:T(8,128)S(1)} %get-tuple-element.8.ortho, f32[256,1024]{1,0:T(8,128)S(1)} %get-tuple-element.9.back, f32[8,256]{1,0:T(8,128)S(1)} %get-tuple-element.10.norm), custom_call_target="tpu_custom_call" | custom-call | tf_op jit(solution)/shard_map/outputs/pallas_call | solution.py:764

commit v8 on v2

--- a/solution.py
+++ b/solution.py
@@ -100,22 +100,44 @@
         for k in range(8 * n)
     ]
     inverse = [jnp.where(lane == sub + 8 * i, 1.0, 0.0) for i in range(n)]
-    for j in range(8 * n):
-        g, r = j // 8, j % 8
-        pivot = row_copy(col[j][g], r)
-        inv = 1.0 / pivot
-        row = row_copy(inverse[g], r)
-        entry = {k: row_copy(col[j][k // 8], k % 8) for k in range(j + 1, 8 * n)}
-        mult = [None if i < g else col[j][i] * inv for i in range(n)]
-        if r < 7:
-            mult[g] = jnp.where(sub > r, mult[g], 0.0)
-        for k in range(j + 1, 8 * n):
+    for g in range(n):
+        entry = [[row_copy(col[8 * g + j][g], i) for j in range(i + 1)] for i in range(8)]
+        rows = [row_copy(inverse[g], j) for j in range(8)]
+        inv, mult = [], [[None] * 8 for _ in range(8)]
+        for j in range(8):
+            inv.append(1.0 / entry[j][j])
+            for k in range(j + 1, 8):
+                mult[k][j] = entry[k][j] * inv[j]
+                for i in range(k, 8):
+                    entry[i][k] = entry[i][k] - entry[i][j] * mult[k][j]
+                rows[k] = rows[k] - mult[k][j] * rows[j]
+        final = jnp.zeros((8, 128), F32)
+        for j in range(8):
+            final = jnp.where(sub == j, rows[j] * lax.rsqrt(entry[j][j]), final)
+        inverse[g] = final
+        below = {}
+        for i in range(g + 1, n):
+            c = [col[8 * g + j][i] for j in range(8)]
+            for j in range(8):
+                for k in range(j + 1, 8):
+                    c[k] = c[k] - c[j] * mult[k][j]
+            below[i] = (c, [c[j] * inv[j] for j in range(8)])
+        for k in range(8 * g + 8, 8 * n):
+            across = [row_copy(below[k // 8][0][j], k % 8) for j in range(8)]
             for i in range(k // 8, n):
-                col[k][i] = col[k][i] - mult[i] * entry[k]
-        for i in range(g + (r == 7), n):
-            inverse[i] = inverse[i] - mult[i] * row
-        inverse[g] = jnp.where(sub == r, row * lax.rsqrt(pivot), inverse[g])
+                for j in range(8):
+                    col[k][i] = col[k][i] - below[i][1][j] * across[j]
+        for i in range(g + 1, n):
+            for j in range(8):
+                inverse[i] = inverse[i] - below[i][1][j] * rows[j]
     return jnp.concatenate(inverse, axis=0)
+
+
+def split3(x):
+    first = x.astype(BF16)
+    rest = x - first.astype(F32)
+    second = rest.astype(BF16)
+    return first, second, (rest - second.astype(F32)).astype(BF16)
 
 
 def eliminate(k, half, m_ref):
@@ -129,9 +151,13 @@
 
     @pl.when(k < 7)
     def _():
-        subl = lax.broadcasted_iota(jnp.int32, (RANK - left, 32), 0)
-        lower = jnp.where(subl >= 32 * k + 32 - left, scaled[:, : RANK - left].T, 0.0)
-        m_ref[left:, cols] -= nn(lower, scaled, HIGH)
+        lane = lax.broadcasted_iota(jnp.int32, (32, RANK - left), 1)
+        lower = jnp.where(lane >= 32 * k + 32 - left, scaled[:, : RANK - left], 0.0)
+        a, b, c = split3(lower)
+        d, e, f = split3(scaled)
+        m_ref[left:, cols] -= tn(
+            jnp.concatenate([a, a, b, a, b, c], axis=0), jnp.concatenate([d, e, d, f, e, d], axis=0)
+        )
 
 
 def main_kernel(
@@ -301,15 +327,14 @@
         def _():
             add_core(2)
             send(part_v.at[5, b_rows], side_v.at[1], N_LEFT_B, right)
+            arrive(hop_v.at[0], N_HOP_A)
+            part_v[5, a_rows] += hop_v[0]
+            send(part_v.at[5, a_rows], side_v.at[0], N_LEFT_A, right)
+            arrive(hop_v.at[1], N_HOP_B)
+            part_v[3, b_rows] += hop_v[1]
+            send(part_v.at[3, b_rows], side_v.at[3], N_RIGHT_B, left)
 
     add_core(3)
-    arrive(hop_v.at[0], N_HOP_A)
-    part_v[5, a_rows] += hop_v[0]
-    send(part_v.at[5, a_rows], side_v.at[0], N_LEFT_A, right)
-    arrive(hop_v.at[1], N_HOP_B)
-    part_v[3, b_rows] += hop_v[1]
-    send(part_v.at[3, b_rows], side_v.at[3], N_RIGHT_B, left)
-
     my_row = piece_row(c, x)
     arrive(side_v.at[2], N_RIGHT_A)
     arrive(side_v.at[0], N_LEFT_A)
@@ -343,12 +368,14 @@
         return pl.ds(pl.multiple_of(row * 8, 8), 8)
 
     def gram_start():
-        gram_part[...] = jnp.zeros((128, RANK), F32)
-
-        @pl.loop(0, 2)
-        def _(core):
+        left, right = [], []
+        for core in range(2):
             rows = pl.ds(piece_row(core, x), PIECE)
-            gram_part[...] += tn(proj[rows, half_cols], proj[rows, :], HIGH)
+            a, b, d = split3(proj[rows, half_cols])
+            left += [a, a, b, a, b, d]
+            a, b, d = split3(proj[rows, :])
+            right += [a, b, a, d, b, a]
+        gram_part[...] = tn(jnp.concatenate(left, axis=0), jnp.concatenate(right, axis=0))
 
         @pl.loop(1, 16)
         def _(d):
@@ -411,21 +438,24 @@
             send_part(xl, 0, G_OPP_A, right)
             arrive(part_of(c, xr, 1), G_RIGHT_B)
             send_part(xr, 1, G_OPP_B, left)
-            gram_across()
             arrive(part_of(c, xr, 0), G_RIGHT_A)
             send_whole(xr, G_CORE + 1)
             arrive(part_of(c, xl, 1), G_LEFT_B)
             send_whole(xl, G_CORE + 2)
 
+        @pl.when(g == 3)
+        def _():
+            gram_across()
+
         @pl.when(g == 4)
         def _():
             arrive(part_of(c, xo, 0), G_OPP_A)
             arrive(part_of(c, xo, 1), G_OPP_B)
             send_whole(xo, G_CORE + 3)
+
+        @pl.when(g == 5)
+        def _():
             gram_round()
-
-        @pl.when(g == 5)
-        def _():
             arrive(whole_of(1 - c, xr), G_CORE + 1)
 
         @pl.when(g == 6)
@@ -434,6 +464,7 @@
 
         @pl.when(g == 7)
         def _():
+            gram_pair()
             arrive(whole_of(1 - c, xo), G_CORE + 3)
 
         rows = pl.ds(piece_row(core, chip), PIECE)
@@ -471,6 +502,10 @@
         kr, kl, ko = (k + 1) % 4, (k + 3) % 4, (k + 2) % 4
         send(w.at[rows32(h, ko), ca], w_hop.at[2 * h], W_HOP + 2 * h, first(kr))
         send(w.at[rows32(h, ko), cb], w_hop.at[2 * h + 1], W_HOP + 2 * h + 1, first(kl))
+
+    def w_step_1b(h):
+        k, q, first, _ = places(h)
+        kr, kl = (k + 1) % 4, (k + 3) % 4
         send(w.at[rows32(h, kr), cb], w_side.at[4 * h + 1], W_NEXT + 4 * h + 1, first(kr))
         send(w.at[rows32(h, kl), ca], w_side.at[4 * h + 2], W_NEXT + 4 * h + 2, first(kl))
 
@@ -545,18 +580,14 @@
         arrive(w_full.at[rows32(h, ko), cb], W_FAR + 2 * h + 1)
 
     def both_halves(step):
-        @pl.loop(0, 2)
-        def _(h):
+        for h in range(2):
             step(h)
 
     both_halves(w_step_1)
-    gram_pair()
-    w_steps_at = (w_step_2, None, w_step_3, w_step_4, None, w_step_5, w_step_6, w_step_7)
-
-    all_sent(N_HOP_A, 12, side_v.at[0])
-    all_sent(N_CORE, 8, part_v.at[0])
-    all_sent(GRAM_SUM, 33, sq_v.at[0])
-    all_sent(GRAM_CORE, 1, gram_part)
+    both_halves(w_step_1b)
+    both_halves(w_step_2)
+    w_steps_at = (w_step_3, None, w_step_4, None, w_step_5, None, w_step_6, w_step_7)
+
     arrive(gram_half(1 - c), GRAM_CORE)
     elim[:, :RANK] = gram[...]
     rr = lax.broadcasted_iota(jnp.int32, (RANK, RANK), 0)
@@ -605,6 +636,10 @@
             jnp.concatenate([first, turned[:, 256:512], first], axis=0),
         )
 
+    all_sent(N_HOP_A, 12, side_v.at[0])
+    all_sent(N_CORE, 8, part_v.at[0])
+    all_sent(GRAM_SUM, 33, sq_v.at[0])
+    all_sent(GRAM_CORE, 1, gram_part)
     all_sent(W_HOP, 24, w_hop.at[0])
     all_sent(W_SUB, 12, w_sub.at[0])
 
@@ -627,14 +662,18 @@
     norms = norm[0:1, :]
 
     def copies(i):
-        rows = pl.ds(pl.multiple_of(i * STEP, 64), STEP)
+        slot = i % 2
+        found = []
+        for p in range(2):
+            rows = pl.ds(pl.multiple_of(i * STEP + p * PIECE, 32), PIECE)
+            here = pl.ds(p * PIECE, PIECE)
+            found.append(pltpu.make_async_copy(mom_v.at[slot, here], mom_out.at[rows], sems.at[slot, p]))
+            found.append(
+                pltpu.make_async_copy(update_v.at[slot, here], update_out.at[rows], sems.at[slot, 2 + p])
+            )
         rank_rows = pl.ds(pl.multiple_of(i * 256, 256), 256)
-        slot = i % 2
-        return (
-            pltpu.make_async_copy(mom_v.at[slot], mom_out.at[rows], sems.at[slot, 0]),
-            pltpu.make_async_copy(update_v.at[slot], update_out.at[rows], sems.at[slot, 1]),
-            pltpu.make_async_copy(basis_v.at[slot], basis_out.at[rank_rows], sems.at[slot, 2]),
-        )
+        found.append(pltpu.make_async_copy(basis_v.at[slot], basis_out.at[rank_rows], sems.at[slot, 4]))
+        return found
 
     @pl.loop(0, LOCAL_ROWS // STEP)
     def _(i):
@@ -650,10 +689,14 @@
         basis_v[slot] = back[:, cols].T * norms
         plain = ortho[rows, :]
         mom_v[slot] = blend[rows, :] - nn((0.05 * plain).astype(BF16), backs[:RANK])
+        mom_a, update_a, mom_b, update_b, basis_copy = copies(i)
+        mom_a.start()
+        mom_b.start(priority=1)
+        basis_copy.start()
         hi, lo = split(plain * (scale * norms))
         update_v[slot] = nn(jnp.concatenate([hi, hi, lo], axis=1), backs[...]).astype(BF16)
-        for copy in copies(i):
-            copy.start()
+        update_a.start()
+        update_b.start(priority=1)
 
     for i in (2, 3):
         for copy in copies(i):
@@ -723,7 +766,7 @@
             vmem((2, STEP, LOCAL_COLS), F32),
             vmem((2, 256, RANK), F32),
             vmem((2, STEP, LOCAL_COLS), BF16),
-            pltpu.SemaphoreType.DMA((2, 3)),
+            pltpu.SemaphoreType.DMA((2, 5)),
         ],
         compiler_params=pltpu.CompilerParams(vmem_limit_bytes=32 * 2**20),
         name="outputs",

time: 71.4 us -> 74.3 us (1.041)
  Pallas kernels: 70.6 us -> 73.6 us
    pallas_call x1, Pallas kernels: 64.9 us -> 67.9 us  [body(): pl.pallas_call(main_kernel, out_shape=(vmem((LOCAL_ROWS, LOCAL_COLS), F32...]
where the time goes in v8:
time: 74.3 us; the launch traced here: 74.2 us
  Pallas kernels  73.6 us (99%)
    pallas_call x1, Pallas kernels, body(): pl.pallas_call(main_kernel, out_shape=(vmem((LOCAL_ROWS, LOCAL_COLS), F32...  67.9 us
    pallas_call x1, Pallas kernels, body(): pl.pallas_call(write_kernel, out_shape=(jax.ShapeDtypeStruct((LOCAL_ROWS,...  5.73 us

profile of v8, /device:TPU:1, one launch (start us, length us, event | category | flops | bytes accessed | tf_op | source)
XLA Modules:
  0.0 74.2 jit_solution(12735719640206897031)
XLA Ops:
  0.6 67.9 %transfers.1 = (f32[1792,1024]{1,0:T(8,128)S(1)}, f32[1792,256]{1,0:T(8,128)S(1)}, f32[256,1024]{1,0:T(8,128)S(1)}, f32[8,256]{1,0:T(8,128)S(1)}) custom-call(bf16[1792,1024]{1,0:T(8,128)(2,1)} %grad.1, f32[1792,1024]{1,0:T(8,128)} %mom.1, f32[1024,256]{1,0:T(8,128)} %basis.1), custom_call_target="tpu_custom_call" | custom-call | tf_op jit(solution)/shard_map/transfers/pallas_call | solution.py:711
  68.5 5.7 %outputs.1 = (f32[1792,1024]{1,0:T(8,128)}, f32[1024,256]{1,0:T(8,128)}, bf16[1792,1024]{1,0:T(8,128)(2,1)}) custom-call(f32[1792,1024]{1,0:T(8,128)S(1)} %get-tuple-element.7.blend, f32[1792,256]{1,0:T(8,128)S(1)} %get-tuple-element.8.ortho, f32[256,1024]{1,0:T(8,128)S(1)} %get-tuple-element.9.back, f32[8,256]{1,0:T(8,128)S(1)} %get-tuple-element.10.norm), custom_call_target="tpu_custom_call" | custom-call | tf_op jit(solution)/shard_map/outputs/pallas_call | solution.py:755

commit v9 on v8

--- a/solution.py
+++ b/solution.py
@@ -431,31 +431,27 @@
         def _():
             arrive(whole_of(1 - c, x), G_CORE)
             gram_start()
-
-        @pl.when(g == 2)
-        def _():
             arrive(part_of(c, xl, 0), G_LEFT_A)
             send_part(xl, 0, G_OPP_A, right)
             arrive(part_of(c, xr, 1), G_RIGHT_B)
             send_part(xr, 1, G_OPP_B, left)
+
+        @pl.when(g == 2)
+        def _():
             arrive(part_of(c, xr, 0), G_RIGHT_A)
             send_whole(xr, G_CORE + 1)
             arrive(part_of(c, xl, 1), G_LEFT_B)
             send_whole(xl, G_CORE + 2)
 
-        @pl.when(g == 3)
-        def _():
-            gram_across()
-
         @pl.when(g == 4)
         def _():
             arrive(part_of(c, xo, 0), G_OPP_A)
             arrive(part_of(c, xo, 1), G_OPP_B)
             send_whole(xo, G_CORE + 3)
+            gram_across()
 
         @pl.when(g == 5)
         def _():
-            gram_round()
             arrive(whole_of(1 - c, xr), G_CORE + 1)
 
         @pl.when(g == 6)
@@ -464,7 +460,6 @@
 
         @pl.when(g == 7)
         def _():
-            gram_pair()
             arrive(whole_of(1 - c, xo), G_CORE + 3)
 
         rows = pl.ds(piece_row(core, chip), PIECE)
@@ -585,8 +580,11 @@
 
     both_halves(w_step_1)
     both_halves(w_step_1b)
+    gram_round()
     both_halves(w_step_2)
-    w_steps_at = (w_step_3, None, w_step_4, None, w_step_5, None, w_step_6, w_step_7)
+    gram_pair()
+    both_halves(w_step_3)
+    w_steps_at = (w_step_4, None, w_step_5, None, w_step_6, None, w_step_7, None)
 
     arrive(gram_half(1 - c), GRAM_CORE)
     elim[:, :RANK] = gram[...]

time: 74.3 us -> 71.6 us (0.964)
  Pallas kernels: 73.6 us -> 70.9 us
    pallas_call x1, Pallas kernels: 67.9 us -> 65.1 us  [body(): pl.pallas_call(main_kernel, out_shape=(vmem((LOCAL_ROWS, LOCAL_COLS), F32...]
where the time goes in v9:
time: 71.6 us; the launch traced here: 71.5 us
  Pallas kernels  70.9 us (99%)
    pallas_call x1, Pallas kernels, body(): pl.pallas_call(main_kernel, out_shape=(vmem((LOCAL_ROWS, LOCAL_COLS), F32...  65.1 us
    pallas_call x1, Pallas kernels, body(): pl.pallas_call(write_kernel, out_shape=(jax.ShapeDtypeStruct((LOCAL_ROWS,...  5.73 us

profile of v9, /device:TPU:1, one launch (start us, length us, event | category | flops | bytes accessed | tf_op | source)
XLA Modules:
  0.0 71.5 jit_solution(14358447199970841920)
XLA Ops:
  0.6 65.1 %transfers.1 = (f32[1792,1024]{1,0:T(8,128)S(1)}, f32[1792,256]{1,0:T(8,128)S(1)}, f32[256,1024]{1,0:T(8,128)S(1)}, f32[8,256]{1,0:T(8,128)S(1)}) custom-call(bf16[1792,1024]{1,0:T(8,128)(2,1)} %grad.1, f32[1792,1024]{1,0:T(8,128)} %mom.1, f32[1024,256]{1,0:T(8,128)} %basis.1), custom_call_target="tpu_custom_call" | custom-call | tf_op jit(solution)/shard_map/transfers/pallas_call | solution.py:709
  65.8 5.7 %outputs.1 = (f32[1792,1024]{1,0:T(8,128)}, f32[1024,256]{1,0:T(8,128)}, bf16[1792,1024]{1,0:T(8,128)(2,1)}) custom-call(f32[1792,1024]{1,0:T(8,128)S(1)} %get-tuple-element.7.blend, f32[1792,256]{1,0:T(8,128)S(1)} %get-tuple-element.8.ortho, f32[256,1024]{1,0:T(8,128)S(1)} %get-tuple-element.9.back, f32[8,256]{1,0:T(8,128)S(1)} %get-tuple-element.10.norm), custom_call_target="tpu_custom_call" | custom-call | tf_op jit(solution)/shard_map/outputs/pallas_call | solution.py:753

commit v10 on v7

--- a/solution.py
+++ b/solution.py
@@ -269,8 +269,7 @@
     basis_copy.wait()
     basis_hi, basis_lo = split(basis_v[...])
     bases[:LOCAL_COLS] = basis_hi
-    bases[LOCAL_COLS : 2 * LOCAL_COLS] = basis_lo
-    bases[2 * LOCAL_COLS :] = basis_hi
+    bases[LOCAL_COLS:] = basis_lo
     turned[...] = jnp.zeros_like(turned)
     hi_v[LOCAL_ROWS:, :] = jnp.zeros((32, LOCAL_COLS), BF16)
     lo_v[LOCAL_ROWS:, :] = jnp.zeros((32, LOCAL_COLS), BF16)
@@ -290,7 +289,8 @@
         hi, lo = split(blend)
         hi_v[rows, :] = hi
         lo_v[rows, :] = lo
-        return nn(jnp.concatenate([hi, hi, lo], axis=1), bases[...])
+        first, second = bases[:LOCAL_COLS], bases[LOCAL_COLS:]
+        return nn(hi, first) + nn(hi, second) + nn(lo, first)
 
     a_rows, b_rows = pl.ds(0, PART), pl.ds(PART, PART)
 
@@ -368,12 +368,14 @@
         return pl.ds(pl.multiple_of(row * 8, 8), 8)
 
     def gram_start():
-        gram_part[...] = jnp.zeros((128, RANK), F32)
-
-        @pl.loop(0, 2)
-        def _(core):
+        halves = []
+        for core in range(2):
             rows = pl.ds(piece_row(core, x), PIECE)
-            gram_part[...] += tn(proj[rows, half_cols], proj[rows, :], HIGH)
+            a, b, d = split3(proj[rows, half_cols])
+            left = jnp.concatenate([a, a, b, a, b, d], axis=0)
+            a, b, d = split3(proj[rows, :])
+            halves.append(tn(left, jnp.concatenate([a, b, a, d, b, a], axis=0)))
+        gram_part[...] = halves[0] + halves[1]
 
         @pl.loop(1, 16)
         def _(d):
@@ -635,15 +637,12 @@
     turned[:, :256] = t_hi
     turned[:, 256:512] = t_lo
 
-    @pl.loop(0, 8)
+    @pl.loop(0, LOCAL_ROWS // STEP)
     def _(i):
-        rows = pl.ds(pl.multiple_of(i * PIECE, 32), PIECE)
+        rows = pl.ds(pl.multiple_of(i * STEP, 64), STEP)
         hi, lo = split(proj[rows, :])
-        first = turned[:, :256]
-        ortho_out[rows, :] = nn(
-            jnp.concatenate([hi, hi, lo], axis=1),
-            jnp.concatenate([first, turned[:, 256:512], first], axis=0),
-        )
+        first, second = turned[:, :256], turned[:, 256:512]
+        ortho_out[rows, :] = nn(hi, first) + nn(hi, second) + nn(lo, first)
 
     all_sent(N_HOP_A, 12, side_v.at[0])
     all_sent(N_CORE, 8, part_v.at[0])
@@ -730,7 +729,7 @@
         scratch_shapes=[
             vmem((4, PIECE, LOCAL_COLS), BF16),
             vmem((LOCAL_COLS, RANK), F32),
-            vmem((3 * LOCAL_COLS, RANK), BF16),
+            vmem((2 * LOCAL_COLS, RANK), BF16),
             vmem((LOCAL_ROWS + 32, LOCAL_COLS), BF16),
             vmem((LOCAL_ROWS + 32, LOCAL_COLS), BF16),
             vmem((8, PIECE, RANK), F32),

time: 70.5 us -> 70.2 us (level)
  no operation moved by 1% of the time
where the time goes in v10:
time: 70.2 us; the launch traced here: 70.1 us
  Pallas kernels  69.5 us (99%)
    pallas_call x1, Pallas kernels, body(): pl.pallas_call(main_kernel, out_shape=(vmem((LOCAL_ROWS, LOCAL_COLS), F32...  63.8 us
    pallas_call x1, Pallas kernels, body(): pl.pallas_call(write_kernel, out_shape=(jax.ShapeDtypeStruct((LOCAL_ROWS,...  5.73 us

profile of v10, /device:TPU:1, one launch (start us, length us, event | category | flops | bytes accessed | tf_op | source)
XLA Modules:
  0.0 70.1 jit_solution(3993563801479390892)
XLA Ops:
  0.6 63.8 %transfers.1 = (f32[1792,1024]{1,0:T(8,128)S(1)}, f32[1792,256]{1,0:T(8,128)S(1)}, f32[256,1024]{1,0:T(8,128)S(1)}, f32[8,256]{1,0:T(8,128)S(1)}) custom-call(bf16[1792,1024]{1,0:T(8,128)(2,1)} %grad.1, f32[1792,1024]{1,0:T(8,128)} %mom.1, f32[1024,256]{1,0:T(8,128)} %basis.1), custom_call_target="tpu_custom_call" | custom-call | tf_op jit(solution)/shard_map/transfers/pallas_call | solution.py:719
  64.4 5.7 %outputs.1 = (f32[1792,1024]{1,0:T(8,128)}, f32[1024,256]{1,0:T(8,128)}, bf16[1792,1024]{1,0:T(8,128)(2,1)}) custom-call(f32[1792,1024]{1,0:T(8,128)S(1)} %get-tuple-element.7.blend, f32[1792,256]{1,0:T(8,128)S(1)} %get-tuple-element.8.ortho, f32[256,1024]{1,0:T(8,128)S(1)} %get-tuple-element.9.back, f32[8,256]{1,0:T(8,128)S(1)} %get-tuple-element.10.norm), custom_call_target="tpu_custom_call" | custom-call | tf_op jit(solution)/shard_map/outputs/pallas_call | solution.py:763

commit v11 on v10

--- a/solution.py
+++ b/solution.py
@@ -92,17 +92,14 @@
 
 
 def inverse_factor(x):
+    x = list(x)
     n = len(x)
     sub = lax.broadcasted_iota(jnp.int32, (8, 128), 0)
-    lane = lax.broadcasted_iota(jnp.int32, (8, 128), 1)
-    col = [
-        [None if i < k // 8 else jnp.broadcast_to(x[i][:, k : k + 1], (8, 128)) for i in range(n)]
-        for k in range(8 * n)
-    ]
-    inverse = [jnp.where(lane == sub + 8 * i, 1.0, 0.0) for i in range(n)]
     for g in range(n):
-        entry = [[row_copy(col[8 * g + j][g], i) for j in range(i + 1)] for i in range(8)]
-        rows = [row_copy(inverse[g], j) for j in range(8)]
+        lanes = [32 + 8 * g + j for j in range(8)]
+        col = {i: [jnp.broadcast_to(x[i][:, at : at + 1], (8, 128)) for at in lanes] for i in range(g, n)}
+        entry = [[row_copy(col[g][j], i) for j in range(i + 1)] for i in range(8)]
+        rows = [row_copy(x[g], j) for j in range(8)]
         inv, mult = [], [[None] * 8 for _ in range(8)]
         for j in range(8):
             inv.append(1.0 / entry[j][j])
@@ -111,26 +108,17 @@
                 for i in range(k, 8):
                     entry[i][k] = entry[i][k] - entry[i][j] * mult[k][j]
                 rows[k] = rows[k] - mult[k][j] * rows[j]
+        for i in range(g + 1, n):
+            c = col[i]
+            for j in range(8):
+                for k in range(j + 1, 8):
+                    c[k] = c[k] - c[j] * mult[k][j]
+                x[i] = x[i] - (c[j] * inv[j]) * rows[j]
         final = jnp.zeros((8, 128), F32)
         for j in range(8):
             final = jnp.where(sub == j, rows[j] * lax.rsqrt(entry[j][j]), final)
-        inverse[g] = final
-        below = {}
-        for i in range(g + 1, n):
-            c = [col[8 * g + j][i] for j in range(8)]
-            for j in range(8):
-                for k in range(j + 1, 8):
-                    c[k] = c[k] - c[j] * mult[k][j]
-            below[i] = (c, [c[j] * inv[j] for j in range(8)])
-        for k in range(8 * g + 8, 8 * n):
-            across = [row_copy(below[k // 8][0][j], k % 8) for j in range(8)]
-            for i in range(k // 8, n):
-                for j in range(8):
-                    col[k][i] = col[k][i] - below[i][1][j] * across[j]
-        for i in range(g + 1, n):
-            for j in range(8):
-                inverse[i] = inverse[i] - below[i][1][j] * rows[j]
-    return jnp.concatenate(inverse, axis=0)
+        x[g] = final
+    return jnp.concatenate(x, axis=0)
 
 
 def split3(x):
@@ -144,8 +132,11 @@
     left = 128 * half
     cols = slice(left, left + 384)
     rows = pl.ds(pl.multiple_of(32 * k, 32), 32)
-    d = pltpu.roll(m_ref[rows, left : left + 128], (128 - 32 * (k % 4)) % 128, 1)
-    inverse = inverse_factor([d[8 * i : 8 * i + 8] for i in range(4)])
+    lane = lax.broadcasted_iota(jnp.int32, (32, 128), 1)
+    subl = lax.broadcasted_iota(jnp.int32, (32, 128), 0)
+    d = pltpu.roll(m_ref[rows, left : left + 128], (160 - 32 * (k % 4)) % 128, 1)
+    x = jnp.where(lane < 32, jnp.where(lane == subl, 1.0, 0.0), d)
+    inverse = inverse_factor([x[8 * i : 8 * i + 8] for i in range(4)])
     scaled = nn(inverse[:, :32], m_ref[rows, cols], HIGH)
     m_ref[rows, cols] = scaled
 

time: 70.2 us -> 70.3 us (level)
  no operation moved by 1% of the time
where the time goes in v11:
time: 70.3 us; the launch traced here: 70.2 us
  Pallas kernels  69.6 us (99%)
    pallas_call x1, Pallas kernels, body(): pl.pallas_call(main_kernel, out_shape=(vmem((LOCAL_ROWS, LOCAL_COLS), F32...  63.9 us
    pallas_call x1, Pallas kernels, body(): pl.pallas_call(write_kernel, out_shape=(jax.ShapeDtypeStruct((LOCAL_ROWS,...  5.73 us

profile of v11, /device:TPU:1, one launch (start us, length us, event | category | flops | bytes accessed | tf_op | source)
XLA Modules:
  0.0 70.2 jit_solution(14926389853981383474)
XLA Ops:
  0.6 63.9 %transfers.1 = (f32[1792,1024]{1,0:T(8,128)S(1)}, f32[1792,256]{1,0:T(8,128)S(1)}, f32[256,1024]{1,0:T(8,128)S(1)}, f32[8,256]{1,0:T(8,128)S(1)}) custom-call(bf16[1792,1024]{1,0:T(8,128)(2,1)} %grad.1, f32[1792,1024]{1,0:T(8,128)} %mom.1, f32[1024,256]{1,0:T(8,128)} %basis.1), custom_call_target="tpu_custom_call" | custom-call | tf_op jit(solution)/shard_map/transfers/pallas_call | solution.py:710
  64.5 5.7 %outputs.1 = (f32[1792,1024]{1,0:T(8,128)}, f32[1024,256]{1,0:T(8,128)}, bf16[1792,1024]{1,0:T(8,128)(2,1)}) custom-call(f32[1792,1024]{1,0:T(8,128)S(1)} %get-tuple-element.7.blend, f32[1792,256]{1,0:T(8,128)S(1)} %get-tuple-element.8.ortho, f32[256,1024]{1,0:T(8,128)S(1)} %get-tuple-element.9.back, f32[8,256]{1,0:T(8,128)S(1)} %get-tuple-element.10.norm), custom_call_target="tpu_custom_call" | custom-call | tf_op jit(solution)/shard_map/outputs/pallas_call | solution.py:754

commit v12 on v8

--- a/solution.py
+++ b/solution.py
@@ -92,17 +92,14 @@
 
 
 def inverse_factor(x):
+    x = list(x)
     n = len(x)
     sub = lax.broadcasted_iota(jnp.int32, (8, 128), 0)
-    lane = lax.broadcasted_iota(jnp.int32, (8, 128), 1)
-    col = [
-        [None if i < k // 8 else jnp.broadcast_to(x[i][:, k : k + 1], (8, 128)) for i in range(n)]
-        for k in range(8 * n)
-    ]
-    inverse = [jnp.where(lane == sub + 8 * i, 1.0, 0.0) for i in range(n)]
     for g in range(n):
-        entry = [[row_copy(col[8 * g + j][g], i) for j in range(i + 1)] for i in range(8)]
-        rows = [row_copy(inverse[g], j) for j in range(8)]
+        lanes = [32 + 8 * g + j for j in range(8)]
+        col = {i: [jnp.broadcast_to(x[i][:, at : at + 1], (8, 128)) for at in lanes] for i in range(g, n)}
+        entry = [[row_copy(col[g][j], i) for j in range(i + 1)] for i in range(8)]
+        rows = [row_copy(x[g], j) for j in range(8)]
         inv, mult = [], [[None] * 8 for _ in range(8)]
         for j in range(8):
             inv.append(1.0 / entry[j][j])
@@ -111,26 +108,17 @@
                 for i in range(k, 8):
                     entry[i][k] = entry[i][k] - entry[i][j] * mult[k][j]
                 rows[k] = rows[k] - mult[k][j] * rows[j]
+        for i in range(g + 1, n):
+            c = col[i]
+            for j in range(8):
+                for k in range(j + 1, 8):
+                    c[k] = c[k] - c[j] * mult[k][j]
+                x[i] = x[i] - (c[j] * inv[j]) * rows[j]
         final = jnp.zeros((8, 128), F32)
         for j in range(8):
             final = jnp.where(sub == j, rows[j] * lax.rsqrt(entry[j][j]), final)
-        inverse[g] = final
-        below = {}
-        for i in range(g + 1, n):
-            c = [col[8 * g + j][i] for j in range(8)]
-            for j in range(8):
-                for k in range(j + 1, 8):
-                    c[k] = c[k] - c[j] * mult[k][j]
-            below[i] = (c, [c[j] * inv[j] for j in range(8)])
-        for k in range(8 * g + 8, 8 * n):
-            across = [row_copy(below[k // 8][0][j], k % 8) for j in range(8)]
-            for i in range(k // 8, n):
-                for j in range(8):
-                    col[k][i] = col[k][i] - below[i][1][j] * across[j]
-        for i in range(g + 1, n):
-            for j in range(8):
-                inverse[i] = inverse[i] - below[i][1][j] * rows[j]
-    return jnp.concatenate(inverse, axis=0)
+        x[g] = final
+    return jnp.concatenate(x, axis=0)
 
 
 def split3(x):
@@ -144,8 +132,11 @@
     left = 128 * half
     cols = slice(left, left + 384)
     rows = pl.ds(pl.multiple_of(32 * k, 32), 32)
-    d = pltpu.roll(m_ref[rows, left : left + 128], (128 - 32 * (k % 4)) % 128, 1)
-    inverse = inverse_factor([d[8 * i : 8 * i + 8] for i in range(4)])
+    lane = lax.broadcasted_iota(jnp.int32, (32, 128), 1)
+    subl = lax.broadcasted_iota(jnp.int32, (32, 128), 0)
+    d = pltpu.roll(m_ref[rows, left : left + 128], (160 - 32 * (k % 4)) % 128, 1)
+    x = jnp.where(lane < 32, jnp.where(lane == subl, 1.0, 0.0), d)
+    inverse = inverse_factor([x[8 * i : 8 * i + 8] for i in range(4)])
     scaled = nn(inverse[:, :32], m_ref[rows, cols], HIGH)
     m_ref[rows, cols] = scaled
 
@@ -269,8 +260,7 @@
     basis_copy.wait()
     basis_hi, basis_lo = split(basis_v[...])
     bases[:LOCAL_COLS] = basis_hi
-    bases[LOCAL_COLS : 2 * LOCAL_COLS] = basis_lo
-    bases[2 * LOCAL_COLS :] = basis_hi
+    bases[LOCAL_COLS:] = basis_lo
     turned[...] = jnp.zeros_like(turned)
     hi_v[LOCAL_ROWS:, :] = jnp.zeros((32, LOCAL_COLS), BF16)
     lo_v[LOCAL_ROWS:, :] = jnp.zeros((32, LOCAL_COLS), BF16)
@@ -290,7 +280,8 @@
         hi, lo = split(blend)
         hi_v[rows, :] = hi
         lo_v[rows, :] = lo
-        return nn(jnp.concatenate([hi, hi, lo], axis=1), bases[...])
+        first, second = bases[:LOCAL_COLS], bases[LOCAL_COLS:]
+        return nn(hi, first) + nn(hi, second) + nn(lo, first)
 
     a_rows, b_rows = pl.ds(0, PART), pl.ds(PART, PART)
 
@@ -455,16 +446,15 @@
 
         @pl.when(g == 5)
         def _():
+            arrive(whole_of(1 - c, xr), G_CORE + 1)
+
+        @pl.when(g == 6)
+        def _():
             gram_round()
-            arrive(whole_of(1 - c, xr), G_CORE + 1)
-
-        @pl.when(g == 6)
-        def _():
             arrive(whole_of(1 - c, xl), G_CORE + 2)
 
         @pl.when(g == 7)
         def _():
-            gram_pair()
             arrive(whole_of(1 - c, xo), G_CORE + 3)
 
         rows = pl.ds(piece_row(core, chip), PIECE)
@@ -586,7 +576,9 @@
     both_halves(w_step_1)
     both_halves(w_step_1b)
     both_halves(w_step_2)
-    w_steps_at = (w_step_3, None, w_step_4, None, w_step_5, None, w_step_6, w_step_7)
+    gram_pair()
+    both_halves(w_step_3)
+    w_steps_at = (w_step_4, None, w_step_5, None, w_step_6, None, w_step_7, None)
 
     arrive(gram_half(1 - c), GRAM_CORE)
     elim[:, :RANK] = gram[...]
@@ -626,15 +618,12 @@
     turned[:, :256] = t_hi
     turned[:, 256:512] = t_lo
 
-    @pl.loop(0, 8)
+    @pl.loop(0, LOCAL_ROWS // STEP)
     def _(i):
-        rows = pl.ds(pl.multiple_of(i * PIECE, 32), PIECE)
+        rows = pl.ds(pl.multiple_of(i * STEP, 64), STEP)
         hi, lo = split(proj[rows, :])
-        first = turned[:, :256]
-        ortho_out[rows, :] = nn(
-            jnp.concatenate([hi, hi, lo], axis=1),
-            jnp.concatenate([first, turned[:, 256:512], first], axis=0),
-        )
+        first, second = turned[:, :256], turned[:, 256:512]
+        ortho_out[rows, :] = nn(hi, first) + nn(hi, second) + nn(lo, first)
 
     all_sent(N_HOP_A, 12, side_v.at[0])
     all_sent(N_CORE, 8, part_v.at[0])
@@ -721,7 +710,7 @@
         scratch_shapes=[
             vmem((4, PIECE, LOCAL_COLS), BF16),
             vmem((LOCAL_COLS, RANK), F32),
-            vmem((3 * LOCAL_COLS, RANK), BF16),
+            vmem((2 * LOCAL_COLS, RANK), BF16),
             vmem((LOCAL_ROWS + 32, LOCAL_COLS), BF16),
             vmem((LOCAL_ROWS + 32, LOCAL_COLS), BF16),
             vmem((8, PIECE, RANK), F32),

time: 74.3 us -> 72 us (0.969)
  Pallas kernels: 73.6 us -> 71.2 us
    pallas_call x1, Pallas kernels: 67.9 us -> 65.5 us  [body(): pl.pallas_call(main_kernel, out_shape=(vmem((LOCAL_ROWS, LOCAL_COLS), F32...]
where the time goes in v12:
time: 72 us; the launch traced here: 71.9 us
  Pallas kernels  71.2 us (99%)
    pallas_call x1, Pallas kernels, body(): pl.pallas_call(main_kernel, out_shape=(vmem((LOCAL_ROWS, LOCAL_COLS), F32...  65.5 us
    pallas_call x1, Pallas kernels, body(): pl.pallas_call(write_kernel, out_shape=(jax.ShapeDtypeStruct((LOCAL_ROWS,...  5.73 us

profile of v12, /device:TPU:1, one launch (start us, length us, event | category | flops | bytes accessed | tf_op | source)
XLA Modules:
  0.0 71.9 jit_solution(1965968252790597928)
XLA Ops:
  0.6 65.5 %transfers.1 = (f32[1792,1024]{1,0:T(8,128)S(1)}, f32[1792,256]{1,0:T(8,128)S(1)}, f32[256,1024]{1,0:T(8,128)S(1)}, f32[8,256]{1,0:T(8,128)S(1)}) custom-call(bf16[1792,1024]{1,0:T(8,128)(2,1)} %grad.1, f32[1792,1024]{1,0:T(8,128)} %mom.1, f32[1024,256]{1,0:T(8,128)} %basis.1), custom_call_target="tpu_custom_call" | custom-call | tf_op jit(solution)/shard_map/transfers/pallas_call | solution.py:700
  66.2 5.7 %outputs.1 = (f32[1792,1024]{1,0:T(8,128)}, f32[1024,256]{1,0:T(8,128)}, bf16[1792,1024]{1,0:T(8,128)(2,1)}) custom-call(f32[1792,1024]{1,0:T(8,128)S(1)} %get-tuple-element.7.blend, f32[1792,256]{1,0:T(8,128)S(1)} %get-tuple-element.8.ortho, f32[256,1024]{1,0:T(8,128)S(1)} %get-tuple-element.9.back, f32[8,256]{1,0:T(8,128)S(1)} %get-tuple-element.10.norm), custom_call_target="tpu_custom_call" | custom-call | tf_op jit(solution)/shard_map/outputs/pallas_call | solution.py:744

commit v13 on v11

--- a/solution.py
+++ b/solution.py
@@ -437,10 +437,10 @@
 
         @pl.when(g == 4)
         def _():
+            gram_round()
             arrive(part_of(c, xo, 0), G_OPP_A)
             arrive(part_of(c, xo, 1), G_OPP_B)
             send_whole(xo, G_CORE + 3)
-            gram_round()
 
         @pl.when(g == 5)
         def _():
@@ -452,6 +452,7 @@
 
         @pl.when(g == 7)
         def _():
+            gram_pair()
             arrive(whole_of(1 - c, xo), G_CORE + 3)
 
         rows = pl.ds(piece_row(core, chip), PIECE)
@@ -586,7 +587,6 @@
             step(i // 2, i % 2)
 
     all_parts(w_step_1)
-    gram_pair()
     all_parts(w_step_2)
     w_steps_at = (w_step_3, None, w_step_4, None, w_step_5, None, w_step_6, w_step_7)
 

time: 70.3 us -> 72.6 us (1.033)
  Pallas kernels: 69.6 us -> 71.8 us
    pallas_call x1, Pallas kernels: 63.9 us -> 66.1 us  [body(): pl.pallas_call(main_kernel, out_shape=(vmem((LOCAL_ROWS, LOCAL_COLS), F32...]
where the time goes in v13:
time: 72.6 us; the launch traced here: 72.4 us
  Pallas kernels  71.8 us (99%)
    pallas_call x1, Pallas kernels, body(): pl.pallas_call(main_kernel, out_shape=(vmem((LOCAL_ROWS, LOCAL_COLS), F32...  66.1 us
    pallas_call x1, Pallas kernels, body(): pl.pallas_call(write_kernel, out_shape=(jax.ShapeDtypeStruct((LOCAL_ROWS,...  5.73 us

profile of v13, /device:TPU:1, one launch (start us, length us, event | category | flops | bytes accessed | tf_op | source)
XLA Modules:
  0.0 72.4 jit_solution(6008149898832212623)
XLA Ops:
  0.6 66.1 %transfers.1 = (f32[1792,1024]{1,0:T(8,128)S(1)}, f32[1792,256]{1,0:T(8,128)S(1)}, f32[256,1024]{1,0:T(8,128)S(1)}, f32[8,256]{1,0:T(8,128)S(1)}) custom-call(bf16[1792,1024]{1,0:T(8,128)(2,1)} %grad.1, f32[1792,1024]{1,0:T(8,128)} %mom.1, f32[1024,256]{1,0:T(8,128)} %basis.1), custom_call_target="tpu_custom_call" | custom-call | tf_op jit(solution)/shard_map/transfers/pallas_call | solution.py:710
  66.7 5.7 %outputs.1 = (f32[1792,1024]{1,0:T(8,128)}, f32[1024,256]{1,0:T(8,128)}, bf16[1792,1024]{1,0:T(8,128)(2,1)}) custom-call(f32[1792,1024]{1,0:T(8,128)S(1)} %get-tuple-element.7.blend, f32[1792,256]{1,0:T(8,128)S(1)} %get-tuple-element.8.ortho, f32[256,1024]{1,0:T(8,128)S(1)} %get-tuple-element.9.back, f32[8,256]{1,0:T(8,128)S(1)} %get-tuple-element.10.norm), custom_call_target="tpu_custom_call" | custom-call | tf_op jit(solution)/shard_map/outputs/pallas_call | solution.py:754

commit v14 on v10

--- a/solution.py
+++ b/solution.py
@@ -597,9 +597,10 @@
     all_parts(w_step_1)
     gram_pair()
     all_parts(w_step_2)
-    w_steps_at = (w_step_3, None, w_step_4, None, w_step_5, None, w_step_6, w_step_7)
+    w_steps_at = (None, w_step_4, None, w_step_5, None, w_step_6, None, w_step_7)
 
     arrive(gram_half(1 - c), GRAM_CORE)
+    all_parts(w_step_3)
     elim[:, :RANK] = gram[...]
     rr = lax.broadcasted_iota(jnp.int32, (RANK, RANK), 0)
     cc = lax.broadcasted_iota(jnp.int32, (RANK, RANK), 1)

time: 70.2 us -> 70.2 us (level)
  no operation moved by 1% of the time
where the time goes in v14:
time: 70.2 us; the launch traced here: 70.1 us
  Pallas kernels  69.4 us (99%)
    pallas_call x1, Pallas kernels, body(): pl.pallas_call(main_kernel, out_shape=(vmem((LOCAL_ROWS, LOCAL_COLS), F32...  63.7 us
    pallas_call x1, Pallas kernels, body(): pl.pallas_call(write_kernel, out_shape=(jax.ShapeDtypeStruct((LOCAL_ROWS,...  5.73 us

profile of v14, /device:TPU:1, one launch (start us, length us, event | category | flops | bytes accessed | tf_op | source)
XLA Modules:
  0.0 70.1 jit_solution(14496844083817890167)
XLA Ops:
  0.6 63.7 %transfers.1 = (f32[1792,1024]{1,0:T(8,128)S(1)}, f32[1792,256]{1,0:T(8,128)S(1)}, f32[256,1024]{1,0:T(8,128)S(1)}, f32[8,256]{1,0:T(8,128)S(1)}) custom-call(bf16[1792,1024]{1,0:T(8,128)(2,1)} %grad.1, f32[1792,1024]{1,0:T(8,128)} %mom.1, f32[1024,256]{1,0:T(8,128)} %basis.1), custom_call_target="tpu_custom_call" | custom-call | tf_op jit(solution)/shard_map/transfers/pallas_call | solution.py:720
  64.3 5.7 %outputs.1 = (f32[1792,1024]{1,0:T(8,128)}, f32[1024,256]{1,0:T(8,128)}, bf16[1792,1024]{1,0:T(8,128)(2,1)}) custom-call(f32[1792,1024]{1,0:T(8,128)S(1)} %get-tuple-element.7.blend, f32[1792,256]{1,0:T(8,128)S(1)} %get-tuple-element.8.ortho, f32[256,1024]{1,0:T(8,128)S(1)} %get-tuple-element.9.back, f32[8,256]{1,0:T(8,128)S(1)} %get-tuple-element.10.norm), custom_call_target="tpu_custom_call" | custom-call | tf_op jit(solution)/shard_map/outputs/pallas_call | solution.py:764

commit v15 on v11

--- a/solution.py
+++ b/solution.py
@@ -588,9 +588,10 @@
     all_parts(w_step_1)
     gram_pair()
     all_parts(w_step_2)
-    w_steps_at = (w_step_3, None, w_step_4, None, w_step_5, None, w_step_6, w_step_7)
+    w_steps_at = (None, w_step_4, None, w_step_5, None, w_step_6, None, w_step_7)
 
     arrive(gram_half(1 - c), GRAM_CORE)
+    all_parts(w_step_3)
     elim[:, :RANK] = gram[...]
     rr = lax.broadcasted_iota(jnp.int32, (RANK, RANK), 0)
     cc = lax.broadcasted_iota(jnp.int32, (RANK, RANK), 1)

time: 70.3 us -> 70.1 us (level)
  no operation moved by 1% of the time
where the time goes in v15:
time: 70.1 us; the launch traced here: 70 us
  Pallas kernels  69.4 us (99%)
    pallas_call x1, Pallas kernels, body(): pl.pallas_call(main_kernel, out_shape=(vmem((LOCAL_ROWS, LOCAL_COLS), F32...  63.7 us
    pallas_call x1, Pallas kernels, body(): pl.pallas_call(write_kernel, out_shape=(jax.ShapeDtypeStruct((LOCAL_ROWS,...  5.73 us

profile of v15, /device:TPU:1, one launch (start us, length us, event | category | flops | bytes accessed | tf_op | source)
XLA Modules:
  0.0 70.0 jit_solution(15378637818032462165)
XLA Ops:
  0.6 63.7 %transfers.1 = (f32[1792,1024]{1,0:T(8,128)S(1)}, f32[1792,256]{1,0:T(8,128)S(1)}, f32[256,1024]{1,0:T(8,128)S(1)}, f32[8,256]{1,0:T(8,128)S(1)}) custom-call(bf16[1792,1024]{1,0:T(8,128)(2,1)} %grad.1, f32[1792,1024]{1,0:T(8,128)} %mom.1, f32[1024,256]{1,0:T(8,128)} %basis.1), custom_call_target="tpu_custom_call" | custom-call | tf_op jit(solution)/shard_map/transfers/pallas_call | solution.py:711
  64.3 5.7 %outputs.1 = (f32[1792,1024]{1,0:T(8,128)}, f32[1024,256]{1,0:T(8,128)}, bf16[1792,1024]{1,0:T(8,128)(2,1)}) custom-call(f32[1792,1024]{1,0:T(8,128)S(1)} %get-tuple-element.7.blend, f32[1792,256]{1,0:T(8,128)S(1)} %get-tuple-element.8.ortho, f32[256,1024]{1,0:T(8,128)S(1)} %get-tuple-element.9.back, f32[8,256]{1,0:T(8,128)S(1)} %get-tuple-element.10.norm), custom_call_target="tpu_custom_call" | custom-call | tf_op jit(solution)/shard_map/outputs/pallas_call | solution.py:755
